TPU v7x, 256 devices: a whole 4x4x8 slice. The times are simulated.
256 devices in a mesh: grp: 4 (over x), cp: 64 (over y, z, core).
Axes of the slice: x: 4, y: 4, z: 8, core: 2. Of those that a mesh axis runs over, the one named last changes fastest.
Arguments:
- queries: bfloat16 [32768, 3072], P(('grp', 'cp')), may hold values from -27 to 27
- keys: bfloat16 [32768, 3072], P(('grp', 'cp')), may hold values from -27 to 27
- values: bfloat16 [32768, 3072], P(('grp', 'cp')), may hold values from -6 to 6
- segment_ids: int32 [32768], P(('grp', 'cp')), may hold values from 0 to 169, never falling along the last dimension, each value on 1 to 384 neighbouring positions
Outputs:
- attended: bfloat16 [32768, 3072], P(('grp', 'cp'))
- log_sum: float32 [24, 32768], P(None, ('grp', 'cp'))
Inputs may be any that keep to these rules, and one draw needn't show every extreme that they name: `segment_ids`: segment ids never fall along the tokens; each segment holds 1 to 384 tokens and one holds exactly 384.
All inputs are finite; a program needn't handle non-finite values.
Results may differ from a plain program's by a relative error of at most 0.009.
Values may be sent and summed in bfloat16 or wider, within the bound.
A program may use at most 64 MiB of HBM per device.

v0:
```python
import jax
import jax.numpy as jnp
from jax import lax
from jax.sharding import PartitionSpec as P

H = 24
FRAME = 128
REACH = 4


def shifted(block, axis, distance):
    devices = range(lax.axis_size(axis))
    route = [(i - distance, i) for i in devices if i - distance in devices]
    return lax.ppermute(block, axis, route)


def fold_block(state, q_block, k_block, v_block, mask):
    top, total, acc = state
    scale = 1.0 / q_block.shape[-1] ** 0.5
    scores = (
        jnp.einsum("qhd,khd->hqk", q_block, k_block, preferred_element_type=jnp.float32) * scale
    )
    scores = jnp.where(mask[None], scores, -jnp.inf)
    new_top = jnp.maximum(top, jnp.max(scores, axis=-1))
    expo = jnp.exp(scores - new_top[..., None])
    factor = jnp.exp(top - new_top)
    total = total * factor + jnp.sum(expo, axis=-1)
    weights = expo.astype(jnp.bfloat16)
    update = jnp.einsum("hqk,khd->qhd", weights, v_block, preferred_element_type=jnp.float32)
    acc = acc * jnp.transpose(factor)[:, :, None] + update
    return (new_top, total, acc)


def shards(queries, keys, values, segment_ids):
    rows = queries.shape[0]
    heads = H
    width = queries.shape[1] // heads
    q_block = queries.reshape(rows, heads, width)
    k_own = keys.reshape(rows, heads, width)
    v_own = values.reshape(rows, heads, width)
    index = lax.axis_index(("grp", "cp"))
    positions = index * rows + jnp.arange(rows, dtype=jnp.int32)
    frames = positions // FRAME
    own_mask = (segment_ids[:, None] == segment_ids[None, :]) & (frames[None, :] <= frames[:, None])
    state = (
        jnp.full((heads, rows), -jnp.inf, jnp.float32),
        jnp.zeros((heads, rows), jnp.float32),
        jnp.zeros((rows, heads, width), jnp.float32),
    )
    state = fold_block(state, q_block, k_own, v_own, own_mask)
    moving_k, moving_v, moving_s = (keys, values, segment_ids)
    for step in range(1, REACH):
        moving_k, moving_v, moving_s = shifted((moving_k, moving_v, moving_s), ("grp", "cp"), 1)
        far_k, far_v, far_s = (moving_k, moving_v, moving_s)
        valid = index - step >= 0
        mask = (segment_ids[:, None] == far_s[None, :]) & valid
        state = fold_block(
            state,
            q_block,
            far_k.reshape(rows, heads, width),
            far_v.reshape(rows, heads, width),
            mask,
        )
    top, total, acc = state
    attended = (
        (acc / jnp.transpose(total)[:, :, None]).astype(jnp.bfloat16).reshape(rows, heads * width)
    )
    return (attended, top + jnp.log(total))


def solution(mesh):
    in_specs = (
        P(("grp", "cp"), None),
        P(("grp", "cp"), None),
        P(("grp", "cp"), None),
        P(("grp", "cp")),
    )
    out_specs = (P(("grp", "cp"), None), P(None, ("grp", "cp")))
    return jax.shard_map(shards, mesh=mesh, in_specs=in_specs, out_specs=out_specs, check_vma=False)
```

profile of v0, /device:TPU:6, one launch (start us, length us, event | category | flops | bytes accessed | tf_op | source)
XLA Modules:
  0.0 104.1 jit_solution(2308149450520039242)
XLA Ops:
  0.6 0.0 copy-start
  0.6 0.0 copy-start.7
  0.7 0.0 copy-start.6
  0.7 0.0 copy-start.8
  0.7 1.7 %copy.24 = bf16[128,3072]{0,1:T(8,128)(2,1)S(1)} copy(bf16[128,3072]{1,0:T(8,128)(2,1)} %param.5) | data formatting | bytes 1572864 | tf_op args[1]
  2.3 1.9 %collective-permute-start.1 = (bf16[128,3072]{0,1:T(8,128)(2,1)S(1)}, bf16[128,3072]{0,1:T(8,128)(2,1)}, u32[]{:S(2)}, u32[]{:S(2)}) collective-permute-start(bf16[128,3072]{0,1:T(8,128)(2,1)S(1)} %copy.24), channel_id=1, source_target_pairs={{0,1},{1,2},{2,3},{3,4},{4,5},{5,6},{6,7},{7,8},{8,9},{9,10},{10,1... | collective-permute-start | bytes 2359304 | tf_op jit(solution)/shard_map/ppermute | solution.py:14
  4.3 0.0 copy-done.6
  4.3 3.9 %collective-permute-start.2 = (bf16[128,3072]{1,0:T(8,128)(2,1)S(1)}, bf16[128,3072]{1,0:T(8,128)(2,1)}, u32[]{:S(2)}, u32[]{:S(2)}) collective-permute-start(bf16[128,3072]{1,0:T(8,128)(2,1)S(1)} %copy-done.6), channel_id=1, source_target_pairs={{0,1},{1,2},{2,3},{3,4},{4,5},{5,6},{6,7},{7,8},{8,9},{9,10},{10,1... | collective-permute-start | bytes 2359304 | tf_op jit(solution)/shard_map/ppermute | solution.py:14
  8.2 13.8 %collective-permute-done.1 = bf16[128,3072]{0,1:T(8,128)(2,1)} collective-permute-done((bf16[128,3072]{0,1:T(8,128)(2,1)S(1)}, bf16[128,3072]{0,1:T(8,128)(2,1)}, u32[]{:S(2)}, u32[]{:S(2)}) %collective-permute-start.1) | collective-permute-done | bytes 786464 | tf_op jit(solution)/shard_map/ppermute | solution.py:14
  22.0 1.9 %collective-permute-start.4 = (bf16[128,3072]{0,1:T(8,128)(2,1)}, bf16[128,3072]{0,1:T(8,128)(2,1)}, u32[]{:S(2)}, u32[]{:S(2)}) collective-permute-start(bf16[128,3072]{0,1:T(8,128)(2,1)} %collective-permute-done.1), channel_id=1, source_target_pairs={{0,1},{1,2},{2,3},{3,4},{4,5},{5,6},{6,7},{7,8},{8,9},{9,10},{10,1... | collective-permute-start | bytes 2359304 | tf_op jit(solution)/shard_map/ppermute | solution.py:14
  23.9 1.9 %collective-permute-start = (s32[128]{0:T(128)}, s32[128]{0:T(128)S(1)}, u32[]{:S(2)}, u32[]{:S(2)}) collective-permute-start(s32[128]{0:T(128)} %param.7), channel_id=1, source_target_pairs={{0,1},{1,2},{2,3},{3,4},{4,5},{5,6},{6,7},{7,8},{8,9},{9,10},{10,1... | collective-permute-start | bytes 1544 | tf_op jit(solution)/shard_map/ppermute | solution.py:14
  25.9 14.0 %collective-permute-done = s32[128]{0:T(128)S(1)} collective-permute-done((s32[128]{0:T(128)}, s32[128]{0:T(128)S(1)}, u32[]{:S(2)}, u32[]{:S(2)}) %collective-permute-start) | collective-permute-done | bytes 544 | tf_op jit(solution)/shard_map/ppermute | solution.py:14
  39.9 1.9 %collective-permute-start.3 = (s32[128]{0:T(128)S(1)}, s32[128]{0:T(128)S(1)}, u32[]{:S(2)}, u32[]{:S(2)}) collective-permute-start(s32[128]{0:T(128)S(1)} %collective-permute-done), channel_id=1, source_target_pairs={{0,1},{1,2},{2,3},{3,4},{4,5},{5,6},{6,7},{7,8},{8,9},{9,10},{10,1... | collective-permute-start | bytes 1544 | tf_op jit(solution)/shard_map/ppermute | solution.py:14
  41.8 0.4 copy.45
  42.2 6.8 %collective-permute-done.3 = s32[128]{0:T(128)S(1)} collective-permute-done((s32[128]{0:T(128)S(1)}, s32[128]{0:T(128)S(1)}, u32[]{:S(2)}, u32[]{:S(2)}) %collective-permute-start.3) | collective-permute-done | bytes 544 | tf_op jit(solution)/shard_map/ppermute | solution.py:14
  48.9 1.9 %collective-permute-start.6 = (s32[128]{0:T(128)S(1)}, s32[128]{0:T(128)S(1)}, u32[]{:S(2)}, u32[]{:S(2)}) collective-permute-start(s32[128]{0:T(128)S(1)} %collective-permute-done.3), channel_id=1, source_target_pairs={{0,1},{1,2},{2,3},{3,4},{4,5},{5,6},{6,7},{7,8},{8,9},{9,10},{10,1... | collective-permute-start | bytes 1544 | tf_op jit(solution)/shard_map/ppermute | solution.py:14
  50.9 7.1 %collective-permute-done.6 = s32[128]{0:T(128)S(1)} collective-permute-done((s32[128]{0:T(128)S(1)}, s32[128]{0:T(128)S(1)}, u32[]{:S(2)}, u32[]{:S(2)}) %collective-permute-start.6) | collective-permute-done | bytes 544 | tf_op jit(solution)/shard_map/ppermute | solution.py:14
  58.0 0.0 copy-done.8
  58.0 0.2 compare_and_fusion.2
  58.2 0.0 collective-permute-done.2
  58.2 1.9 %collective-permute-start.5 = (bf16[128,3072]{1,0:T(8,128)(2,1)}, bf16[128,3072]{1,0:T(8,128)(2,1)}, u32[]{:S(2)}, u32[]{:S(2)}) collective-permute-start(bf16[128,3072]{1,0:T(8,128)(2,1)} %collective-permute-done.2), channel_id=1, source_target_pairs={{0,1},{1,2},{2,3},{3,4},{4,5},{5,6},{6,7},{7,8},{8,9},{9,10},{10,1... | collective-permute-start | bytes 2359304 | tf_op jit(solution)/shard_map/ppermute | solution.py:14
  60.1 0.0 copy-done
  60.1 0.0 copy-done.7
  60.1 0.7 fusion.65
  60.8 0.0 copy-start.3
  60.8 0.0 collective-permute-done.4
  60.8 1.9 %collective-permute-start.7 = (bf16[128,3072]{0,1:T(8,128)(2,1)}, bf16[128,3072]{0,1:T(8,128)(2,1)}, u32[]{:S(2)}, u32[]{:S(2)}) collective-permute-start(bf16[128,3072]{0,1:T(8,128)(2,1)} %collective-permute-done.4), channel_id=1, source_target_pairs={{0,1},{1,2},{2,3},{3,4},{4,5},{5,6},{6,7},{7,8},{8,9},{9,10},{10,1... | collective-permute-start | bytes 2359304 | tf_op jit(solution)/shard_map/ppermute | solution.py:14
  62.8 0.0 copy-done.3
  62.8 1.6 %fusion.21 = f32[24,128,128]{1,2,0:T(8,128)} fusion(bf16[128,24,128]{0,2,1:T(8,128)(2,1)S(1)} %bitcast.142, f32[24,128,128]{1,2,0:T(8,128)S(1)} %get-tuple-element.23, f32[24,128]{1,0:T(8,128)S(1)} %get-tuple-element.22), kind=kOutput, calls=%fused_computation.30 | convolution fusion | flops 101449728 | bytes 3944448 | tf_op jit(solution)/shard_map/hqk,khd->qhd/dot_general | solution.py:29
  64.3 1.5 %copy.27 = bf16[128,3072]{0,1:T(8,128)(2,1)S(1)} copy(bf16[128,3072]{1,0:T(8,128)(2,1)} %collective-permute-done.2) | data formatting | bytes 1572864 | tf_op jit(solution)/shard_map/ppermute | solution.py:14
  65.8 1.8 %fusion.7 = (f32[24,128]{1,0:T(8,128)S(1)}, f32[24,128,128]{1,2,0:T(8,128)S(1)}) fusion(pred[128,128]{0,1:T(8,128)(4,1)S(1)} %get-tuple-element.14, bf16[128,24,128]{0,2,1:T(8,128)(2,1)} %bitcast.3, bf16[128,3072]{1,0:T(8,128)(2,1)S(1)} %copy-done), kind=kOutput, calls=%fused_computation.19 | convolution fusion | flops 101839872 | bytes 3174400 | tf_op jit(solution)/shard_map/qhd,khd->hqk/dot_general | solution.py:21
  67.7 8.3 %collective-permute-done.5 = bf16[128,3072]{1,0:T(8,128)(2,1)} collective-permute-done((bf16[128,3072]{1,0:T(8,128)(2,1)}, bf16[128,3072]{1,0:T(8,128)(2,1)}, u32[]{:S(2)}, u32[]{:S(2)}) %collective-permute-start.5) | collective-permute-done | bytes 786464 | tf_op jit(solution)/shard_map/ppermute | solution.py:14
  76.0 2.3 %copy.31 = bf16[128,3072]{0,1:T(8,128)(2,1)} copy(bf16[128,3072]{1,0:T(8,128)(2,1)} %collective-permute-done.5) | data formatting | bytes 1572864 | tf_op jit(solution)/shard_map/ppermute | solution.py:14
  78.3 1.9 %collective-permute-start.8 = (bf16[128,3072]{1,0:T(8,128)(2,1)}, bf16[128,3072]{1,0:T(8,128)(2,1)}, u32[]{:S(2)}, u32[]{:S(2)}) collective-permute-start(bf16[128,3072]{1,0:T(8,128)(2,1)} %collective-permute-done.5), channel_id=1, source_target_pairs={{0,1},{1,2},{2,3},{3,4},{4,5},{5,6},{6,7},{7,8},{8,9},{9,10},{10,1... | collective-permute-start | bytes 2359304 | tf_op jit(solution)/shard_map/ppermute | solution.py:14
  80.2 1.8 %fusion.8 = (f32[24,128]{1,0:T(8,128)S(1)}, f32[24,128,128]{1,2,0:T(8,128)S(1)}) fusion(pred[128,128]{0,1:T(8,128)(4,1)S(1)} %get-tuple-element.15, bf16[128,24,128]{0,2,1:T(8,128)(2,1)} %bitcast.7, bf16[128,3072]{1,0:T(8,128)(2,1)S(1)} %copy-done), kind=kOutput, calls=%fused_computation.20 | convolution fusion | flops 101839872 | bytes 3174400 | tf_op jit(solution)/shard_map/qhd,khd->hqk/dot_general | solution.py:21
  82.1 2.4 %collective-permute-done.7 = bf16[128,3072]{0,1:T(8,128)(2,1)} collective-permute-done((bf16[128,3072]{0,1:T(8,128)(2,1)}, bf16[128,3072]{0,1:T(8,128)(2,1)}, u32[]{:S(2)}, u32[]{:S(2)}) %collective-permute-start.7) | collective-permute-done | bytes 786464 | tf_op jit(solution)/shard_map/ppermute | solution.py:14
  84.4 1.9 %fusion.9 = (f32[24,128]{1,0:T(8,128)S(1)}, f32[24,128,128]{1,2,0:T(8,128)S(1)}) fusion(pred[128,128]{0,1:T(8,128)(4,1)S(1)} %get-tuple-element.16, bf16[128,24,128]{0,2,1:T(8,128)(2,1)} %bitcast.11, bf16[128,3072]{1,0:T(8,128)(2,1)S(1)} %copy-done), kind=kOutput, calls=%fused_computation.21 | convolution fusion | flops 101839872 | bytes 3174400 | tf_op jit(solution)/shard_map/qhd,khd->hqk/dot_general | solution.py:21
  86.4 0.0 copy-start.1
  86.4 0.7 fusion.5
  87.1 0.4 copy-done.1
  87.6 0.8 fusion.10
  88.4 0.6 log_add_fusion
  89.0 1.7 %fusion.19 = f32[24,128,128]{1,2,0:T(8,128)} fusion(bf16[128,24,128]{0,2,1:T(8,128)(2,1)S(1)} %bitcast.141, f32[24,128,128]{1,2,0:T(8,128)S(1)} %get-tuple-element.25, f32[24,128]{1,0:T(8,128)S(1)} %get-tuple-element.12, pred[128,128]{0,1:T(8,128)(4,1)S(1)} %get-tuple-element.14), kind=kOutput, calls=%fused_computation.29 | convolution fusion | flops 102236160 | bytes 3960832 | tf_op jit(solution)/shard_map/hqk,khd->qhd/dot_general | solution.py:29
  90.7 1.7 %fusion.17 = f32[24,128,128]{1,2,0:T(8,128)} fusion(bf16[128,24,128]{0,2,1:T(8,128)(2,1)S(1)} %bitcast.143, f32[24,128,128]{1,2,0:T(8,128)S(1)} %get-tuple-element.21, f32[24,128]{1,0:T(8,128)S(1)} %get-tuple-element.11, pred[128,128]{0,1:T(8,128)(4,1)S(1)} %get-tuple-element.15), kind=kOutput, calls=%fused_computation.28 | convolution fusion | flops 102236160 | bytes 3960832 | tf_op jit(solution)/shard_map/hqk,khd->qhd/dot_general | solution.py:29
  92.4 3.7 %collective-permute-done.8 = bf16[128,3072]{1,0:T(8,128)(2,1)} collective-permute-done((bf16[128,3072]{1,0:T(8,128)(2,1)}, bf16[128,3072]{1,0:T(8,128)(2,1)}, u32[]{:S(2)}, u32[]{:S(2)}) %collective-permute-start.8) | collective-permute-done | bytes 786464 | tf_op jit(solution)/shard_map/ppermute | solution.py:14
  96.1 1.5 %copy.35 = bf16[128,3072]{0,1:T(8,128)(2,1)S(1)} copy(bf16[128,3072]{1,0:T(8,128)(2,1)} %collective-permute-done.8) | data formatting | bytes 1572864 | tf_op jit(solution)/shard_map/ppermute | solution.py:14
  97.7 4.1 %fusion.1 = bf16[128,24,128]{0,2,1:T(8,128)(2,1)} fusion(f32[24,128,128]{1,2,0:T(8,128)} %fusion.17, f32[24,128,128]{1,2,0:T(8,128)} %fusion.19, f32[24,128,128]{1,2,0:T(8,128)} %fusion.21, bf16[128,24,128]{0,2,1:T(8,128)(2,1)S(1)} %bitcast.144, f32[24,128,128]{1,2,0:T(8,128)S(1)} %copy-done.2, f32[128,24]{0,1:T(8,128)S(1)} %get-tuple-element.6, ...), kind=kOutput, calls=%fused_computation.2 | convolution fusion | flops 105775104 | bytes 7954432 | tf_op jit(solution)/shard_map/hqk,khd->qhd/dot_general | solution.py:29
  101.8 2.3 %copy.37 = bf16[128,3072]{1,0:T(8,128)(2,1)} copy(bf16[128,3072]{0,1:T(8,128)(2,1)} %bitcast.145) | data formatting | bytes 1572864
  (9 shorter events, 0.1 us)
Async XLA Ops:
  0.6 59.5 %copy-start = (bf16[128,3072]{1,0:T(8,128)(2,1)S(1)}, bf16[128,3072]{1,0:T(8,128)(2,1)}, u32[]{:S(2)}) copy-start(bf16[128,3072]{1,0:T(8,128)(2,1)} %param.4) | copy-start | bytes 2359300
  0.6 59.5 %copy-start.7 = (bf16[128,3072]{1,0:T(8,128)(2,1)S(1)}, bf16[128,3072]{1,0:T(8,128)(2,1)}, u32[]{:S(2)}) copy-start(bf16[128,3072]{1,0:T(8,128)(2,1)} %param.5) | copy-start | bytes 2359300
  0.7 3.6 %copy-start.6 = (bf16[128,3072]{1,0:T(8,128)(2,1)S(1)}, bf16[128,3072]{1,0:T(8,128)(2,1)}, u32[]{:S(2)}) copy-start(bf16[128,3072]{1,0:T(8,128)(2,1)} %param.6) | copy-start | bytes 2359300
  0.7 57.3 %copy-start.8 = (s32[128]{0:T(128)S(1)}, s32[128]{0:T(128)}, u32[]{:S(2)}) copy-start(s32[128]{0:T(128)} %param.7) | copy-start | bytes 1540
  2.3 19.7 %collective-permute-start.1 = (bf16[128,3072]{0,1:T(8,128)(2,1)S(1)}, bf16[128,3072]{0,1:T(8,128)(2,1)}, u32[]{:S(2)}, u32[]{:S(2)}) collective-permute-start(bf16[128,3072]{0,1:T(8,128)(2,1)S(1)} %copy.24), channel_id=1, source_target_pairs={{0,1},{1,2},{2,3},{3,4},{4,5},{5,6},{6,7},{7,8},{8,9},{9,10},{10,1... | collective-permute-start | bytes 2359304 | tf_op jit(solution)/shard_map/ppermute | solution.py:14
  4.3 53.9 %collective-permute-start.2 = (bf16[128,3072]{1,0:T(8,128)(2,1)S(1)}, bf16[128,3072]{1,0:T(8,128)(2,1)}, u32[]{:S(2)}, u32[]{:S(2)}) collective-permute-start(bf16[128,3072]{1,0:T(8,128)(2,1)S(1)} %copy-done.6), channel_id=1, source_target_pairs={{0,1},{1,2},{2,3},{3,4},{4,5},{5,6},{6,7},{7,8},{8,9},{9,10},{10,1... | collective-permute-start | bytes 2359304 | tf_op jit(solution)/shard_map/ppermute | solution.py:14
  22.0 38.8 %collective-permute-start.4 = (bf16[128,3072]{0,1:T(8,128)(2,1)}, bf16[128,3072]{0,1:T(8,128)(2,1)}, u32[]{:S(2)}, u32[]{:S(2)}) collective-permute-start(bf16[128,3072]{0,1:T(8,128)(2,1)} %collective-permute-done.1), channel_id=1, source_target_pairs={{0,1},{1,2},{2,3},{3,4},{4,5},{5,6},{6,7},{7,8},{8,9},{9,10},{10,1... | collective-permute-start | bytes 2359304 | tf_op jit(solution)/shard_map/ppermute | solution.py:14
  23.9 15.9 %collective-permute-start = (s32[128]{0:T(128)}, s32[128]{0:T(128)S(1)}, u32[]{:S(2)}, u32[]{:S(2)}) collective-permute-start(s32[128]{0:T(128)} %param.7), channel_id=1, source_target_pairs={{0,1},{1,2},{2,3},{3,4},{4,5},{5,6},{6,7},{7,8},{8,9},{9,10},{10,1... | collective-permute-start | bytes 1544 | tf_op jit(solution)/shard_map/ppermute | solution.py:14
  39.9 9.1 %collective-permute-start.3 = (s32[128]{0:T(128)S(1)}, s32[128]{0:T(128)S(1)}, u32[]{:S(2)}, u32[]{:S(2)}) collective-permute-start(s32[128]{0:T(128)S(1)} %collective-permute-done), channel_id=1, source_target_pairs={{0,1},{1,2},{2,3},{3,4},{4,5},{5,6},{6,7},{7,8},{8,9},{9,10},{10,1... | collective-permute-start | bytes 1544 | tf_op jit(solution)/shard_map/ppermute | solution.py:14
  48.9 9.1 %collective-permute-start.6 = (s32[128]{0:T(128)S(1)}, s32[128]{0:T(128)S(1)}, u32[]{:S(2)}, u32[]{:S(2)}) collective-permute-start(s32[128]{0:T(128)S(1)} %collective-permute-done.3), channel_id=1, source_target_pairs={{0,1},{1,2},{2,3},{3,4},{4,5},{5,6},{6,7},{7,8},{8,9},{9,10},{10,1... | collective-permute-start | bytes 1544 | tf_op jit(solution)/shard_map/ppermute | solution.py:14
  58.2 17.8 %collective-permute-start.5 = (bf16[128,3072]{1,0:T(8,128)(2,1)}, bf16[128,3072]{1,0:T(8,128)(2,1)}, u32[]{:S(2)}, u32[]{:S(2)}) collective-permute-start(bf16[128,3072]{1,0:T(8,128)(2,1)} %collective-permute-done.2), channel_id=1, source_target_pairs={{0,1},{1,2},{2,3},{3,4},{4,5},{5,6},{6,7},{7,8},{8,9},{9,10},{10,1... | collective-permute-start | bytes 2359304 | tf_op jit(solution)/shard_map/ppermute | solution.py:14
  60.8 2.0 %copy-start.3 = (f32[24,128,128]{1,2,0:T(8,128)}, f32[24,128,128]{1,2,0:T(8,128)S(1)}, u32[]{:S(2)}) copy-start(f32[24,128,128]{1,2,0:T(8,128)S(1)} %get-tuple-element.23) | copy-start | bytes 4718596
  60.8 23.6 %collective-permute-start.7 = (bf16[128,3072]{0,1:T(8,128)(2,1)}, bf16[128,3072]{0,1:T(8,128)(2,1)}, u32[]{:S(2)}, u32[]{:S(2)}) collective-permute-start(bf16[128,3072]{0,1:T(8,128)(2,1)} %collective-permute-done.4), channel_id=1, source_target_pairs={{0,1},{1,2},{2,3},{3,4},{4,5},{5,6},{6,7},{7,8},{8,9},{9,10},{10,1... | collective-permute-start | bytes 2359304 | tf_op jit(solution)/shard_map/ppermute | solution.py:14
  78.3 17.8 %collective-permute-start.8 = (bf16[128,3072]{1,0:T(8,128)(2,1)}, bf16[128,3072]{1,0:T(8,128)(2,1)}, u32[]{:S(2)}, u32[]{:S(2)}) collective-permute-start(bf16[128,3072]{1,0:T(8,128)(2,1)} %collective-permute-done.5), channel_id=1, source_target_pairs={{0,1},{1,2},{2,3},{3,4},{4,5},{5,6},{6,7},{7,8},{8,9},{9,10},{10,1... | collective-permute-start | bytes 2359304 | tf_op jit(solution)/shard_map/ppermute | solution.py:14
  84.4 2.0 %copy-start.4 = (f32[24,128,128]{1,2,0:T(8,128)S(1)}, f32[24,128,128]{1,2,0:T(8,128)}, u32[]{:S(2)}) copy-start(f32[24,128,128]{1,2,0:T(8,128)} %copy-done.3) | copy-start | bytes 4718596
  86.4 1.2 %copy-start.1 = (f32[24,128,128]{1,2,0:T(8,128)}, f32[24,128,128]{1,2,0:T(8,128)S(1)}, u32[]{:S(2)}) copy-start(f32[24,128,128]{1,2,0:T(8,128)S(1)} %get-tuple-element.19) | copy-start | bytes 4718596
  89.0 1.7 %copy-start.5 = (bf16[128,3072]{0,1:T(8,128)(2,1)S(1)}, bf16[128,3072]{0,1:T(8,128)(2,1)}, u32[]{:S(2)}) copy-start(bf16[128,3072]{0,1:T(8,128)(2,1)} %copy.31) | copy-start | bytes 2359300
  92.4 5.2 %copy-start.2 = (f32[24,128,128]{1,2,0:T(8,128)S(1)}, f32[24,128,128]{1,2,0:T(8,128)}, u32[]{:S(2)}) copy-start(f32[24,128,128]{1,2,0:T(8,128)} %copy-done.1) | copy-start | bytes 4718596
where the time goes:
time: 105 us; the launch traced here: 104 us
  waiting for transfers between devices  56.1 us (53%)
  starting transfers between devices  19.3 us (18%)
  matrix products  15.4 us (15%)
  local copies, waits for them, and re-layouts  10.1 us (10%)
  other arithmetic  2.31 us (2%)
    ppermute x9, waiting for transfers between devices, shifted(): return lax.ppermute(block, axis, route)  56.1 us
    ppermute x9, starting transfers between devices, shifted(): return lax.ppermute(block, axis, route)  19.3 us
    dot_general x4, matrix products, fold_block(): jnp.einsum('hqk,khd->qhd', weights, v_block, preferred_element_type=jnp.f...  9.09 us
    dot_general x4, matrix products, fold_block(): jnp.einsum('qhd,khd->hqk', q_block, k_block, preferred_element_type=jnp.f...  6.28 us
    ppermute x3, local copies, waits for them, and re-layouts, shifted(): return lax.ppermute(block, axis, route)  5.29 us
    unnamed x20, local copies, waits for them, and re-layouts  4.42 us
  transfers between devices with their start and end apart: 9, of which 7 were waited for; matrix products, arithmetic and copies ran while one was open for 17% of the time, Pallas kernels for 0%

commit v1 on v0

v1 whole, which is shorter than its diff:
```python
import functools
import math

import jax
import jax.numpy as jnp
from jax import lax
from jax.experimental import pallas as pl
from jax.experimental.pallas import tpu as pltpu
from jax.sharding import PartitionSpec as P

T = 128
HALF = T // 2
D = 128
HIDDEN = -1e30
SCALE = 1.0 / math.sqrt(D)
C2 = SCALE / math.log(2.0)
LN2 = math.log(2.0)
MESH = pl.DeviceIdType.MESH
F32 = jnp.float32
BF16 = jnp.bfloat16

QG = 2
OG = 4
LATE = 3


def wide(h):
    return pl.ds(pl.multiple_of(h * D, D), D)


def attend(q, k, v, bias):
    s = lax.dot_general(q, k, (((1,), (1,)), ((), ())), preferred_element_type=F32) + bias
    top = jnp.max(s, axis=1, keepdims=True)
    p = jnp.exp2((s - top) * C2).astype(BF16)
    ext = jnp.concatenate([v, jnp.ones(v.shape, BF16)], axis=1)
    o = lax.dot_general(p, ext, (((1,), (0,)), ((), ())), preferred_element_type=F32)
    total = o[:, D:]
    return o[:, :D] / total, top * C2 + jnp.log2(total)


def kernel(
    n,
    ncp,
    nh,
    q_ref,
    k_ref,
    v_ref,
    id_ref,
    out_ref,
    sum_ref,
    ids,
    q2,
    k2,
    v2,
    qg,
    qf,
    ek,
    ev,
    m_send,
    m_recv,
    l_send,
    l_recv,
    lse_send,
    lse_recv,
    bias_g,
    bias_f,
    bias_o,
    o_loc,
    s_loc,
    stage,
    sums,
    sums_in,
    id_ss,
    id_rs,
    lo_s,
    sib_ss,
    sib_rs,
    e_ss,
    e_rs,
    q_ss,
    qg_rs,
    qf_rs,
    m_ss,
    m_rs,
    l_ss,
    l_rs,
    lse_ss,
    lse_rs,
    out_s,
    oo_ss,
    oo_rs,
    sum_ss,
    sum_rs,
):
    w = nh * D
    ng = nh // QG
    no = nh // OG
    me = lax.axis_index("grp") * ncp + lax.axis_index("cp")
    core = lax.rem(me, 2)
    first = me - core
    other = 1 - core

    def at(i):
        i = lax.rem(i + n, n)
        return (i // ncp, lax.rem(i, ncp))

    sib = at(first + other)
    right = [at(first + 2), at(first + 3)]
    left = [at(first - 2), at(first - 1)]
    ahead = at(me + 2)

    def remote(src, dst, ss, rs, to):
        return pltpu.make_async_remote_copy(
            src_ref=src, dst_ref=dst, send_sem=ss, recv_sem=rs, device_id=to, device_id_type=MESH
        )

    barrier = pltpu.get_barrier_semaphore()
    for to in (sib, *right, *left):
        pl.semaphore_signal(barrier, inc=1, device_id=to, device_id_type=MESH)

    mine = pl.ds(pl.multiple_of(core * w, D), w)
    its = pl.ds(pl.multiple_of(other * w, D), w)
    my_rows = pl.ds(pl.multiple_of(core * T, T), T)
    local = [
        pltpu.make_async_copy(a.at[:, mine], b.at[my_rows, :], lo_s.at[i])
        for i, (a, b) in enumerate(((k_ref, k2), (v_ref, v2), (q_ref, q2)))
    ]
    for cp in local:
        cp.start()
    pl.semaphore_wait(barrier, 5)

    id_sends = []
    for i, (to, slot) in enumerate(
        (
            (sib, 2 + core),
            (right[0], core),
            (right[1], core),
            (left[0], 4 + core),
            (left[1], 4 + core),
        )
    ):
        cp = remote(id_ref, ids.at[slot], id_ss.at[i], id_rs.at[slot], to)
        cp.start()
        id_sends.append(cp)

    def e_copies():
        made = []
        for kk in range(2):
            cols = pl.ds(kk * w, w)
            for i, (a, b) in enumerate(((k_ref, ek), (v_ref, ev))):
                made.append(
                    remote(a.at[pl.ds(HALF, HALF), cols], b, e_ss.at[kk, i], e_rs.at[i], right[kk])
                )
        return made

    def q_copy(g, kk, dst, rs):
        cols = pl.ds(pl.multiple_of((kk * nh + g * QG) * D, D), QG * D)
        here = pl.ds(pl.multiple_of(g * QG * D, D), QG * D)
        return remote(
            q_ref.at[:, cols], dst.at[:, here], q_ss.at[kk, g], rs.at[g], left[kk]
        )

    @pl.when(core == 1)
    def _():
        for g in range(ng):
            for kk in range(2):
                q_copy(g, kk, qg, qg_rs).start()

    sib_sends = [
        remote(a.at[:, its], b.at[my_rows, :], sib_ss.at[i], sib_rs.at[i], sib)
        for i, (a, b) in enumerate(((k_ref, k2), (v_ref, v2), (q_ref, q2)))
    ]
    for cp in sib_sends:
        cp.start()

    @pl.when(core == 1)
    def _():
        for cp in e_copies():
            cp.start()

    ids[2 + core] = id_ref[...]
    for slot in (0, 1, 2 + other, 4, 5):
        remote(id_ref, ids.at[slot], id_ss.at[0], id_rs.at[slot], sib).wait_recv()

    row = [ids[i].astype(F32) for i in range(6)]
    last = [jnp.max(r, axis=1, keepdims=True) for r in row]
    eye = lax.broadcasted_iota(jnp.int32, (T, T), 0) == lax.broadcasted_iota(jnp.int32, (T, T), 1)

    def to_column(r):
        return jnp.sum(jnp.where(eye, jnp.broadcast_to(r, (T, T)), 0.0), axis=1, keepdims=True)

    def to_row(x):
        return jnp.sum(jnp.where(eye, jnp.broadcast_to(x, (T, T)), 0.0), axis=0, keepdims=True)

    def bias_of(q_col, k_row):
        return jnp.where(q_col == k_row, 0.0, HIDDEN)

    behind = jnp.where(last[0] != last[1], row[1], -1.0)
    col = [None, None] + [to_column(row[i]) for i in range(2, 6)]
    for j, keys in enumerate((behind, row[2], row[3])):
        cols = pl.ds(j * T, T)
        bias_f[:, cols] = bias_of(col[4], keys)
        if j:
            bias_g[:, pl.ds((j - 1) * T, T)] = bias_of(col[5], keys)
        bias_o[pl.ds(0, T), cols] = (
            bias_of(col[2], keys) if j < 2 else jnp.full((T, T), HIDDEN, F32)
        )
        bias_o[pl.ds(T, T), cols] = bias_of(col[3], keys)

    kv_row = jnp.broadcast_to(jnp.where(last[2] != last[3], 1.0, 0.0), (1, D))

    for cp in local:
        cp.wait()
    for i, b in enumerate((k2, v2, q2)):
        remote(b.at[my_rows, :], b.at[my_rows, :], sib_ss.at[i], sib_rs.at[i], sib).wait_recv()

    def m_copy(h):
        return remote(m_send.at[h], m_recv.at[h], m_ss.at[h], m_rs.at[h], ahead)

    def l_copy(h):
        return remote(l_send.at[h], l_recv.at[h], l_ss.at[h], l_rs.at[h], ahead)

    def lse_copy(i):
        return remote(lse_send.at[i], lse_recv.at[i], lse_ss.at[i], lse_rs.at[i], ahead)

    def q_wait(g, dst, rs):
        here = pl.ds(pl.multiple_of(g * QG * D, D), QG * D)
        remote(dst.at[:, here], dst.at[:, here], q_ss.at[0, g], rs.at[g], sib).wait_recv()

    def serve_g(g, _):
        q_wait(g, qg, qg_rs)

        @pl.when((core == 0) & (g == LATE))
        def _():
            for gg in range(ng):
                for kk in range(2):
                    q_copy(gg, kk, qf, qf_rs).start()

        kv = kv_row > 0.5
        for u in range(QG):
            h = g * QG + u
            o, lse = attend(qg[:, wide(h)], k2[:, wide(h)], v2[:, wide(h)], bias_g[...])
            lse_send[0, pl.ds(h, 1), :] = jnp.where(kv, HIDDEN, to_row(lse))
            raw = jnp.concatenate(
                [k2[pl.ds(T, HALF), wide(h)], v2[pl.ds(T, HALF), wide(h)]], axis=0
            )
            m_send[h] = jnp.where(kv, raw.astype(F32), o).astype(BF16)
            m_copy(h).start()
        return 0

    lax.fori_loop(0, ng, serve_g, 0)
    lse_copy(0).start()

    remote(ek, ek, e_ss.at[0, 0], e_rs.at[0], sib).wait_recv()
    remote(ev, ev, e_ss.at[0, 1], e_rs.at[1], sib).wait_recv()

    def serve_f(g, _):
        q_wait(g, qf, qf_rs)
        for u in range(QG):
            m_copy(g * QG + u).wait_recv()
        keys, vals = [], []
        for u in range(QG):
            h = g * QG + u
            got = m_recv[h]
            keys.append(jnp.concatenate([got[:HALF], ek[:, wide(h)], k2[:, wide(h)]], axis=0))
            vals.append(jnp.concatenate([got[HALF:], ev[:, wide(h)], v2[:, wide(h)]], axis=0))
        kv = kv_row > 0.5
        for u in range(QG):
            h = g * QG + u
            o, lse = attend(qf[:, wide(h)], keys[u], vals[u], bias_f[...])
            lse_send[1, pl.ds(h, 1), :] = jnp.where(kv, HIDDEN, to_row(lse))
            l_send[h] = o.astype(BF16)
            l_copy(h).start()
        for u in range(QG):
            h = g * QG + u
            o, lse = attend(q2[:, wide(h)], keys[u], vals[u], bias_o[...])
            o_loc[h] = o
            s_loc[h] = lse
        return 0

    lax.fori_loop(0, ng, serve_f, 0)
    lse_copy(1).start()

    def merge(side, h, theirs, got):
        rows = pl.ds(side * T, T)
        here = s_loc[h, rows, :]
        there = to_column(got)
        top = jnp.maximum(here, there)
        a, b = jnp.exp2(here - top), jnp.exp2(there - top)
        both = a + b
        r = 1.0 / both
        out = o_loc[h, rows, :] * (a * r) + theirs.astype(F32) * (b * r)
        stage[side, :, wide(h)] = out.astype(BF16)
        sums[side, pl.ds(h, 1), :] = to_row((top + jnp.log2(both)) * LN2)

    def put(side, g, act):
        cols = pl.ds(g * OG * D, OG * D)
        to = pl.ds(pl.multiple_of(core * w + g * OG * D, D), OG * D)

        @pl.when(core == side)
        def _():
            act(pltpu.make_async_copy(stage.at[side, :, cols], out_ref.at[:, to], out_s.at[g]))

        @pl.when(core != side)
        def _():
            act(
                remote(stage.at[side, :, cols], out_ref.at[:, to], oo_ss.at[g], oo_rs.at[g], sib),
                True,
            )

    def start(cp, far=False):
        cp.start()

    def sent(cp, far=False):
        if far:
            cp.wait_send()
        else:
            cp.wait()

    lse_copy(0).wait_recv()
    for g in range(no):

        def one(i, _):
            h = g * OG + i
            merge(1, h, m_recv[h], lse_recv[0, pl.ds(h, 1), :])
            return 0

        lax.fori_loop(0, OG, one, 0)
        put(1, g, start)

    lse_copy(1).wait_recv()
    for g in range(no):

        def one(i, _):
            h = g * OG + i
            l_copy(h).wait_recv()
            merge(0, h, l_recv[h], lse_recv[1, pl.ds(h, 1), :])
            return 0

        lax.fori_loop(0, OG, one, 0)
        put(0, g, start)

    sum_copy = remote(sums.at[other], sums_in, sum_ss, sum_rs, sib)
    sum_copy.start()

    for cp in id_sends + sib_sends:
        cp.wait_send()

    @pl.when(core == 1)
    def _():
        for cp in e_copies():
            cp.wait_send()
        for g in range(ng):
            for kk in range(2):
                q_copy(g, kk, qg, qg_rs).wait_send()

    @pl.when(core == 0)
    def _():
        for g in range(ng):
            for kk in range(2):
                q_copy(g, kk, qf, qf_rs).wait_send()

    def drain(h, _):
        m_copy(h).wait_send()
        l_copy(h).wait_send()
        return 0

    lax.fori_loop(0, nh, drain, 0)
    lse_copy(0).wait_send()
    lse_copy(1).wait_send()
    sum_copy.wait()

    @pl.when(core == 0)
    def _():
        sum_ref[pl.ds(0, nh), :] = sums[0, pl.ds(0, nh), :]
        sum_ref[pl.ds(nh, nh), :] = sums_in[pl.ds(0, nh), :]

    @pl.when(core == 1)
    def _():
        sum_ref[pl.ds(0, nh), :] = sums_in[pl.ds(0, nh), :]
        sum_ref[pl.ds(nh, nh), :] = sums[1, pl.ds(0, nh), :]

    for g in range(no):
        put(1, g, sent)
        put(0, g, sent)
        to = pl.ds(pl.multiple_of(other * w + g * OG * D, D), OG * D)
        remote(out_ref.at[:, to], out_ref.at[:, to], oo_ss.at[g], oo_rs.at[g], sib).wait_recv()


def shards(mesh, queries, keys, values, segment_ids):
    n, ncp = mesh.size, mesh.shape["cp"]
    width = queries.shape[1]
    heads = width // D
    nh = heads // 2
    ng, no = nh // QG, nh // OG
    w = nh * D
    pad = -(-nh // 8) * 8
    dma = pltpu.SemaphoreType.DMA
    scratch = [
        pltpu.VMEM((6, 1, T), jnp.int32),
        pltpu.VMEM((2 * T, w), BF16),
        pltpu.VMEM((2 * T, w), BF16),
        pltpu.VMEM((2 * T, w), BF16),
        pltpu.VMEM((T, w), BF16),
        pltpu.VMEM((T, w), BF16),
        pltpu.VMEM((HALF, w), BF16),
        pltpu.VMEM((HALF, w), BF16),
        pltpu.VMEM((nh, T, D), BF16),
        pltpu.VMEM((nh, T, D), BF16),
        pltpu.VMEM((nh, T, D), BF16),
        pltpu.VMEM((nh, T, D), BF16),
        pltpu.VMEM((2, pad, T), F32),
        pltpu.VMEM((2, pad, T), F32),
        pltpu.VMEM((T, 2 * T), F32),
        pltpu.VMEM((T, 3 * T), F32),
        pltpu.VMEM((2 * T, 3 * T), F32),
        pltpu.VMEM((nh, 2 * T, D), F32),
        pltpu.VMEM((nh, 2 * T, D), F32),
        pltpu.VMEM((2, T, w), BF16),
        pltpu.VMEM((2, pad, T), F32),
        pltpu.VMEM((pad, T), F32),
        dma((5,)),
        dma((6,)),
        dma((3,)),
        dma((3,)),
        dma((3,)),
        dma((2, 2)),
        dma((2,)),
        dma((2, ng)),
        dma((ng,)),
        dma((ng,)),
        dma((nh,)),
        dma((nh,)),
        dma((nh,)),
        dma((nh,)),
        dma((2,)),
        dma((2,)),
        dma((no,)),
        dma((no,)),
        dma((no,)),
        dma,
        dma,
    ]
    anywhere = pl.BlockSpec(memory_space=pl.ANY)
    vmem = pl.BlockSpec(memory_space=pltpu.VMEM)
    return pl.pallas_call(
        functools.partial(kernel, n, ncp, nh),
        out_shape=(
            jax.ShapeDtypeStruct((T, width), BF16),
            jax.ShapeDtypeStruct((heads, T), F32),
        ),
        in_specs=[anywhere, anywhere, anywhere, vmem],
        out_specs=(anywhere, vmem),
        scratch_shapes=scratch,
        compiler_params=pltpu.CompilerParams(
            collective_id=0, has_side_effects=True, vmem_limit_bytes=48 * 2**20
        ),
        cost_estimate=pl.CostEstimate(
            flops=heads * T * T * D * 20, bytes_accessed=8 * T * width, transcendentals=0
        ),
    )(queries, keys, values, segment_ids.reshape(1, T))


def solution(mesh):
    both = ("grp", "cp")
    return jax.shard_map(
        functools.partial(shards, mesh),
        mesh=mesh,
        in_specs=(P(both, None), P(both, None), P(both, None), P(both)),
        out_specs=(P(both, None), P(None, both)),
        check_vma=False,
    )
```

time: 105 us -> 53.1 us (0.51)
  the two profiles are of different devices: /device:TPU:6 before, /device:TPU:1 now
where the time goes in v1:
time: 53.1 us; the launch traced here: 52.8 us
  Pallas kernels  46.7 us (88%)
  local copies, waits for them, and re-layouts  5.53 us (10%)
  between operations  0.65 us (1%)
    pallas_call x1, Pallas kernels, shards(): pl.pallas_call(functools.partial(kernel, n, ncp, nh), out_shape=(jax.Shap...  46.7 us
    unnamed x10, local copies, waits for them, and re-layouts  5.53 us

profile of v1, /device:TPU:1, one launch (start us, length us, event | category | flops | bytes accessed | tf_op | source)
XLA Modules:
  0.0 52.8 jit_solution(1455931535091239922)
XLA Ops:
  0.6 0.0 copy-start.3
  0.6 0.6 %copy-done.3 = s32[128]{0:T(128)S(1)} copy-done((s32[128]{0:T(128)S(1)}, s32[128]{0:T(128)}, u32[]{:S(2)}) %copy-start.3) | copy-done | bytes 536
  1.3 0.0 copy-start
  1.3 1.1 %copy-done = bf16[128,3072]{1,0:T(8,128)(2,1)S(1)} copy-done((bf16[128,3072]{1,0:T(8,128)(2,1)S(1)}, bf16[128,3072]{1,0:T(8,128)(2,1)}, u32[]{:S(2)}) %copy-start) | copy-done | bytes 786456
  2.4 0.0 copy-start.1
  2.4 1.1 %copy-done.1 = bf16[128,3072]{1,0:T(8,128)(2,1)S(1)} copy-done((bf16[128,3072]{1,0:T(8,128)(2,1)S(1)}, bf16[128,3072]{1,0:T(8,128)(2,1)}, u32[]{:S(2)}) %copy-start.1) | copy-done | bytes 786456
  3.6 0.0 copy-start.2
  3.6 1.1 %copy-done.2 = bf16[128,3072]{1,0:T(8,128)(2,1)S(1)} copy-done((bf16[128,3072]{1,0:T(8,128)(2,1)S(1)}, bf16[128,3072]{1,0:T(8,128)(2,1)}, u32[]{:S(2)}) %copy-start.2) | copy-done | bytes 786456
  4.7 46.7 %shard_map.59 = (bf16[128,3072]{1,0:T(8,128)(2,1)S(1)}, f32[24,128]{1,0:T(8,128)S(1)}) custom-call(bf16[128,3072]{1,0:T(8,128)(2,1)S(1)} %copy-done, bf16[128,3072]{1,0:T(8,128)(2,1)S(1)} %copy-done.1, bf16[128,3072]{1,0:T(8,128)(2,1)S(1)} %copy-done.2, s32[1,128]{1,0:T(1,128)S(1)} %bitcast.1), custom_call_target="tpu_custom_call" | custom-call | flops 1006632960 | bytes 3145728 | tf_op jit(solution)/shard_map/pallas_call | solution.py:446
  51.4 0.9 %copy.8 = bf16[128,3072]{1,0:T(8,128)(2,1)} copy(bf16[128,3072]{1,0:T(8,128)(2,1)S(1)} %get-tuple-element.4) | data formatting | bytes 1572864
  52.2 0.6 %copy.9 = f32[24,128]{1,0:T(8,128)} copy(f32[24,128]{1,0:T(8,128)S(1)} %get-tuple-element.5) | data formatting | bytes 24576
Async XLA Ops:
  0.6 0.7 %copy-start.3 = (s32[128]{0:T(128)S(1)}, s32[128]{0:T(128)}, u32[]{:S(2)}) copy-start(s32[128]{0:T(128)} %param.7) | copy-start | bytes 1540
  1.3 1.1 %copy-start = (bf16[128,3072]{1,0:T(8,128)(2,1)S(1)}, bf16[128,3072]{1,0:T(8,128)(2,1)}, u32[]{:S(2)}) copy-start(bf16[128,3072]{1,0:T(8,128)(2,1)} %q_ref.1) | copy-start | bytes 2359300
  2.4 1.1 %copy-start.1 = (bf16[128,3072]{1,0:T(8,128)(2,1)S(1)}, bf16[128,3072]{1,0:T(8,128)(2,1)}, u32[]{:S(2)}) copy-start(bf16[128,3072]{1,0:T(8,128)(2,1)} %k_ref.1) | copy-start | bytes 2359300
  3.6 1.1 %copy-start.2 = (bf16[128,3072]{1,0:T(8,128)(2,1)S(1)}, bf16[128,3072]{1,0:T(8,128)(2,1)}, u32[]{:S(2)}) copy-start(bf16[128,3072]{1,0:T(8,128)(2,1)} %v_ref.1) | copy-start | bytes 2359300

commit v2 on v1

v2 whole, which is shorter than its diff:
```python
import functools
import math

import jax
import jax.numpy as jnp
from jax import lax
from jax.experimental import pallas as pl
from jax.experimental.pallas import tpu as pltpu
from jax.sharding import PartitionSpec as P

T = 128
HALF = T // 2
PART = T // 4
D = 128
HIDDEN = -1e30
C2 = 1.0 / math.sqrt(D) / math.log(2.0)
LN2 = math.log(2.0)
MESH = pl.DeviceIdType.MESH
F32 = jnp.float32
BF16 = jnp.bfloat16

QG = 2
OG = 4
LATE = 3


def wide(h):
    return pl.ds(pl.multiple_of(h * D, D), D)


def scores(q, k, bias):
    return lax.dot_general(q, k, (((1,), (1,)), ((), ())), preferred_element_type=F32) + bias


def weigh(p, v):
    ext = jnp.concatenate([v, jnp.ones(v.shape, BF16)], axis=1)
    return lax.dot_general(p, ext, (((1,), (0,)), ((), ())), preferred_element_type=F32)


def attend(q, k, v, bias):
    s = scores(q, k, bias)
    top = jnp.max(s, axis=1, keepdims=True)
    o = weigh(jnp.exp2((s - top) * C2).astype(BF16), v)
    return o[:, :D] / o[:, D:], top * C2 + jnp.log2(o[:, D:])


def kernel(
    n,
    ncp,
    nh,
    q_ref,
    k_ref,
    v_ref,
    id_ref,
    out_ref,
    sum_ref,
    ids,
    q2,
    k2,
    v2,
    qg,
    qf,
    ek,
    ev,
    m_send,
    m_recv,
    l_send,
    l_recv,
    lse_send,
    lse_recv,
    bias_g,
    bias_f,
    bias_o,
    bias_b,
    raw,
    tops,
    o_loc,
    s_loc,
    stage,
    sums,
    go,
    id_ss,
    id_rs,
    lo_s,
    sib_ss,
    sib_rs,
    e_ss,
    e_rs,
    qg_ss,
    qg_rs,
    qf_ss,
    qf_rs,
    m_ss,
    m_rs,
    l_ss,
    l_rs,
    lse_ss,
    lse_rs,
    oo_ss,
    oo_rs,
    sum_ss,
    sum_rs,
):
    w = nh * D
    ng = nh // QG
    no = nh // OG
    me = lax.axis_index("grp") * ncp + lax.axis_index("cp")
    core = lax.rem(me, 2)
    first = me - core
    other = 1 - core
    has_left = first > 0
    has_right = first < n - 2

    def at(i):
        i = lax.rem(i + n, n)
        return (i // ncp, lax.rem(i, ncp))

    sib = at(first + other)
    right = [at(first + 2), at(first + 3)]
    left = [at(first - 2), at(first - 1)]
    ahead = at(me + 2)

    def remote(src, dst, ss, rs, to):
        return pltpu.make_async_remote_copy(
            src_ref=src, dst_ref=dst, send_sem=ss, recv_sem=rs, device_id=to, device_id_type=MESH
        )

    def greet(sem, to):
        pl.semaphore_signal(sem, inc=1, device_id=to, device_id_type=MESH)

    def arrived(dst, rs):
        remote(dst, dst, sum_ss.at[0], rs, sib).wait_recv()

    barrier = pltpu.get_barrier_semaphore()
    greet(barrier, sib)

    @pl.when(has_left)
    def _():
        greet(barrier, left[0])
        greet(barrier, left[1])

    mine = pl.ds(pl.multiple_of(core * w, D), w)
    its = pl.ds(pl.multiple_of(other * w, D), w)
    my_rows = pl.ds(pl.multiple_of(core * T, T), T)
    its_rows = pl.ds(pl.multiple_of(other * T, T), T)
    trio = ((k_ref, k2), (v_ref, v2), (q_ref, q2))
    local = [
        pltpu.make_async_copy(a.at[:, mine], b.at[my_rows, :], lo_s.at[i])
        for i, (a, b) in enumerate(trio)
    ]
    local.append(pltpu.make_async_copy(id_ref, ids.at[2 + core], lo_s.at[3]))
    for cp in local:
        cp.start()
    pl.semaphore_wait(barrier, 1 + 2 * has_right.astype(jnp.int32))

    @pl.when(has_right)
    def _():
        greet(go, right[0])
        greet(go, right[1])

    id_sib = remote(id_ref, ids.at[2 + core], id_ss.at[0], id_rs.at[2 + core], sib)
    id_right = [
        remote(id_ref, ids.at[core], id_ss.at[1 + i], id_rs.at[core], right[i]) for i in range(2)
    ]
    id_left = [
        remote(id_ref, ids.at[4 + core], id_ss.at[3 + i], id_rs.at[4 + core], left[i])
        for i in range(2)
    ]
    sib_sends = [
        remote(a.at[:, its], b.at[my_rows, :], sib_ss.at[i], sib_rs.at[i], sib)
        for i, (a, b) in enumerate(trio)
    ]

    def e_copies():
        return [
            remote(
                a.at[pl.ds(T - PART, PART), pl.ds(kk * w, w)], b, e_ss.at[kk, i], e_rs.at[i], right[kk]
            )
            for kk in range(2)
            for i, (a, b) in enumerate(((k_ref, ek), (v_ref, ev)))
        ]

    def q_cols(g):
        return pl.ds(pl.multiple_of(g * QG * D, D), QG * D)

    def qg_copy(g, kk):
        cols = pl.ds(pl.multiple_of((kk * nh + g * QG) * D, D), QG * D)
        return remote(
            q_ref.at[:, cols], qg.at[:, q_cols(g)], qg_ss.at[kk, g], qg_rs.at[g], left[kk]
        )

    def qf_copy(part, g, kk):
        cols = pl.ds(pl.multiple_of((kk * nh + g * QG) * D, D), QG * D)
        rows = pl.ds(part * HALF, HALF)
        return remote(
            q_ref.at[rows, cols],
            qf.at[rows, q_cols(g)],
            qf_ss.at[part, kk, g],
            qf_rs.at[part, g],
            left[kk],
        )

    sib_sends[0].start()

    @pl.when(has_right)
    def _():
        id_right[0].start()
        id_right[1].start()

        @pl.when(core == 1)
        def _():
            for cp in e_copies():
                cp.start()

    id_sib.start()
    sib_sends[1].start()

    @pl.when(has_left)
    def _():
        pl.semaphore_wait(go, 2)
        id_left[0].start()
        id_left[1].start()

        @pl.when(core == 1)
        def _():
            for g in range(ng):
                for kk in range(2):
                    qg_copy(g, kk).start()

    sib_sends[2].start()

    @pl.when(jnp.logical_not(has_left))
    def _():
        ids[0] = jnp.full((1, T), -1, jnp.int32)
        ids[1] = jnp.full((1, T), -1, jnp.int32)
        ek[...] = jnp.zeros(ek.shape, BF16)
        ev[...] = jnp.zeros(ev.shape, BF16)
        m_recv[...] = jnp.zeros(m_recv.shape, BF16)
        l_recv[...] = jnp.zeros(l_recv.shape, BF16)
        lse_recv[...] = jnp.full(lse_recv.shape, HIDDEN, F32)

    @pl.when(jnp.logical_not(has_right))
    def _():
        ids[4] = jnp.full((1, T), -2, jnp.int32)
        ids[5] = jnp.full((1, T), -2, jnp.int32)

    def iota(shape, axis):
        return lax.broadcasted_iota(jnp.int32, shape, axis)

    eye = iota((T, T), 0) == iota((T, T), 1)
    eyes = [iota((HALF, T), 0) + HALF * i == iota((HALF, T), 1) for i in range(2)]

    def to_column(r, like):
        return jnp.sum(
            jnp.where(like, jnp.broadcast_to(r, like.shape), 0.0), axis=1, keepdims=True
        )

    def to_row(x, like):
        return jnp.sum(jnp.where(like, x, 0.0), axis=0, keepdims=True)

    def bias_of(q_col, k_row):
        return jnp.where(q_col == k_row, 0.0, HIDDEN)

    arrived(ids.at[2 + other], id_rs.at[2 + other])
    local[3].wait()
    own = [ids[2].astype(F32), ids[3].astype(F32)]
    own_col = [to_column(r, eye) for r in own]
    for i in range(2):
        for j in range(2):
            bias_o[pl.ds(i * T, T), pl.ds(j * T, T)] = (
                bias_of(own_col[i], own[j]) if j <= i else jnp.full((T, T), HIDDEN, F32)
            )

    last = [jnp.max(r, axis=1, keepdims=True) for r in own]
    kv_row = jnp.broadcast_to(jnp.where(last[0] != last[1], 1.0, 0.0), (1, D))

    @pl.when(has_right)
    def _():
        arrived(ids.at[4], id_rs.at[4])
        arrived(ids.at[5], id_rs.at[5])

    its_col = [to_column(ids[4 + i].astype(F32), eye) for i in range(2)]
    for j in range(2):
        bias_g[:, pl.ds(j * T, T)] = bias_of(its_col[1], own[j])
        bias_f[:, pl.ds((j + 1) * T, T)] = bias_of(its_col[0], own[j])

    for cp in local[:3]:
        cp.wait()
    for i, b in enumerate((k2, v2, q2)):
        arrived(b.at[its_rows, :], sib_rs.at[i])

    def m_copy(h):
        return remote(m_send.at[h], m_recv.at[h], m_ss.at[h], m_rs.at[h], ahead)

    def l_copy(part, h):
        return remote(
            l_send.at[part, h], l_recv.at[part, h], l_ss.at[part, h], l_rs.at[part, h], ahead
        )

    def lse_copy(i):
        return remote(lse_send.at[i], lse_recv.at[i], lse_ss.at[i], lse_rs.at[i], ahead)

    def step_g(g, _):
        @pl.when(has_right)
        def _():
            arrived(qg.at[:, q_cols(g)], qg_rs.at[g])

        @pl.when(has_left & (core == 0) & (g == LATE))
        def _():
            for part in (1, 0):
                for gg in range(ng):
                    for kk in range(2):
                        qf_copy(part, gg, kk).start()

        kv = kv_row > 0.5
        for u in range(QG):
            h = g * QG + u
            o, lse = attend(qg[:, wide(h)], k2[:, wide(h)], v2[:, wide(h)], bias_g[...])
            lse_send[0, pl.ds(h, 1), :] = jnp.where(kv, HIDDEN, to_row(lse, eye))
            rows = pl.ds(T + PART, HALF)
            there = jnp.concatenate([k2[rows, wide(h)], v2[rows, wide(h)]], axis=0)
            m_send[h] = jnp.where(kv, there.astype(F32), o).astype(BF16)

            @pl.when(has_right)
            def _():
                m_copy(h).start()

        for u in range(QG):
            h = g * QG + u
            s = scores(q2[:, wide(h)], k2[:, wide(h)], bias_o[...])
            top = jnp.max(s, axis=1, keepdims=True)
            raw[h] = weigh(jnp.exp2((s - top) * C2).astype(BF16), v2[:, wide(h)])
            tops[h] = jnp.broadcast_to(top, (2 * T, D))
        return 0

    lax.fori_loop(0, ng, step_g, 0)

    @pl.when(has_right)
    def _():
        lse_copy(0).start()

    @pl.when(has_left)
    def _():
        arrived(ids.at[0], id_rs.at[0])
        arrived(ids.at[1], id_rs.at[1])
        arrived(ek, e_rs.at[0])
        arrived(ev, e_rs.at[1])

    before = [ids[i].astype(F32) for i in range(2)]
    behind_last = [jnp.max(r, axis=1, keepdims=True) for r in before]
    behind = jnp.where(behind_last[0] != behind_last[1], before[1], -1.0)
    for i in range(2):
        bias_b[pl.ds(i * T, T), :] = bias_of(own_col[i], behind)
    late = (iota((T, T), 0) >= HALF) & (iota((T, T), 1) < PART)
    bias_f[:, pl.ds(0, T)] = jnp.where(late, HIDDEN, bias_of(its_col[0], behind))

    def step_f1(g, _):
        @pl.when(has_right)
        def _():
            arrived(qf.at[pl.ds(HALF, HALF), q_cols(g)], qf_rs.at[1, g])

        @pl.when(has_left)
        def _():
            for u in range(QG):
                arrived(m_recv.at[g * QG + u], m_rs.at[g * QG + u])

        kv = kv_row > 0.5
        none = jnp.zeros((PART, D), BF16)
        for u in range(QG):
            h = g * QG + u
            got = m_recv[h]
            keys = jnp.concatenate([none, got[:HALF], ek[:, wide(h)], k2[:, wide(h)]], axis=0)
            vals = jnp.concatenate([none, got[HALF:], ev[:, wide(h)], v2[:, wide(h)]], axis=0)
            o, lse = attend(
                qf[pl.ds(HALF, HALF), wide(h)], keys, vals, bias_f[pl.ds(HALF, HALF), :]
            )
            lse_send[1, pl.ds(h, 1), :] = jnp.where(kv, HIDDEN, to_row(lse, eyes[1]))
            rows = pl.ds(T, PART)
            there = jnp.concatenate([k2[rows, wide(h)], v2[rows, wide(h)]], axis=0)
            l_send[1, h] = jnp.where(kv, there.astype(F32), o).astype(BF16)

            @pl.when(has_right)
            def _():
                l_copy(1, h).start()

        return 0

    lax.fori_loop(0, ng, step_f1, 0)

    @pl.when(has_right)
    def _():
        lse_copy(1).start()

    def step_f0(g, _):
        @pl.when(has_right)
        def _():
            arrived(qf.at[pl.ds(0, HALF), q_cols(g)], qf_rs.at[0, g])

        @pl.when(has_left)
        def _():
            for u in range(QG):
                arrived(l_recv.at[1, g * QG + u], l_rs.at[1, g * QG + u])

        kv = kv_row > 0.5
        keys, vals = [], []
        for u in range(QG):
            h = g * QG + u
            low, got = l_recv[1, h], m_recv[h]
            keys.append(jnp.concatenate([low[:PART], got[:HALF], ek[:, wide(h)]], axis=0))
            vals.append(jnp.concatenate([low[PART:], got[HALF:], ev[:, wide(h)]], axis=0))
        for u in range(QG):
            h = g * QG + u
            o, lse = attend(
                qf[pl.ds(0, HALF), wide(h)],
                jnp.concatenate([keys[u], k2[:, wide(h)]], axis=0),
                jnp.concatenate([vals[u], v2[:, wide(h)]], axis=0),
                bias_f[pl.ds(0, HALF), :],
            )
            lse_send[2, pl.ds(h, 1), :] = jnp.where(kv, HIDDEN, to_row(lse, eyes[0]))
            l_send[0, h] = o.astype(BF16)

            @pl.when(has_right)
            def _():
                l_copy(0, h).start()

        for u in range(QG):
            h = g * QG + u
            s = scores(q2[:, wide(h)], keys[u], bias_b[...])
            old = tops[h]
            top = jnp.maximum(old, jnp.max(s, axis=1, keepdims=True))
            fade = jnp.exp2((old - top) * C2)
            new = weigh(jnp.exp2((s - top) * C2).astype(BF16), vals[u])
            total = raw[h, :, pl.ds(D, D)] * fade + new[:, D:]
            o_loc[h] = (raw[h, :, pl.ds(0, D)] * fade + new[:, :D]) / total
            s_loc[h] = top * C2 + jnp.log2(total)
        return 0

    lax.fori_loop(0, ng, step_f0, 0)

    @pl.when(has_right)
    def _():
        lse_copy(2).start()

    def merge(side, start, size, h, theirs, got, like):
        rows = pl.ds(side * T + start, size)
        here = s_loc[h, rows, :]
        there = to_column(got, like)
        top = jnp.maximum(here, there)
        a, b = jnp.exp2(here - top), jnp.exp2(there - top)
        both = a + b
        r = 1.0 / both
        out = o_loc[h, rows, :] * (a * r) + theirs.astype(F32) * (b * r)
        stage[side, pl.ds(start, size), wide(h)] = out.astype(BF16)
        return to_row((top + jnp.log2(both)) * LN2, like)

    def put(slot, side, start, size, g, heads, act):
        rows = pl.ds(start, size)
        cols = pl.ds(g * heads * D, heads * D)
        to = pl.ds(pl.multiple_of(core * w + g * heads * D, D), heads * D)
        src, dst = stage.at[side, rows, cols], out_ref.at[rows, to]

        @pl.when(core == side)
        def _():
            act(pltpu.make_async_copy(src, dst, oo_ss.at[slot]), False)

        @pl.when(core != side)
        def _():
            act(remote(src, dst, oo_ss.at[slot], oo_rs.at[slot], sib), True)

    def begin(cp, far):
        cp.start()

    def sent(cp, far):
        if far:
            cp.wait_send()
        else:
            cp.wait()

    puts = [(0, 1, 0, T, 0, nh), (1, 0, HALF, HALF, 0, nh)] + [
        (2 + g, 0, 0, HALF, g, OG) for g in range(no)
    ]

    @pl.when(has_left)
    def _():
        arrived(lse_recv.at[0], lse_rs.at[0])
        arrived(lse_recv.at[1], lse_rs.at[1])

    def step_e(h, _):
        sums[1, pl.ds(h, 1), :] = merge(
            1, 0, T, h, m_recv[h], lse_recv[0, pl.ds(h, 1), :], eye
        )
        sums[0, pl.ds(h, 1), :] = merge(
            0, HALF, HALF, h, l_recv[1, h], lse_recv[1, pl.ds(h, 1), :], eyes[1]
        )
        return 0

    lax.fori_loop(0, nh, step_e, 0)
    put(*puts[0], begin)
    put(*puts[1], begin)

    @pl.when(has_left)
    def _():
        arrived(lse_recv.at[2], lse_rs.at[2])

    for g in range(no):

        def step_d(i, _):
            h = g * OG + i

            @pl.when(has_left)
            def _():
                arrived(l_recv.at[0, h], l_rs.at[0, h])

            sums[0, pl.ds(h, 1), :] += merge(
                0, 0, HALF, h, l_recv[0, h], lse_recv[2, pl.ds(h, 1), :], eyes[0]
            )
            return 0

        lax.fori_loop(0, OG, step_d, 0)
        put(*puts[2 + g], begin)

    own_sum = pltpu.make_async_copy(sums.at[core], sum_ref.at[core], sum_ss.at[0])
    far_sum = remote(sums.at[other], sum_ref.at[core], sum_ss.at[1], sum_rs, sib)
    own_sum.start()
    far_sum.start()

    id_sib.wait_send()
    for cp in sib_sends:
        cp.wait_send()

    @pl.when(has_right)
    def _():
        for cp in id_right:
            cp.wait_send()

        @pl.when(core == 1)
        def _():
            for cp in e_copies():
                cp.wait_send()

        def drain(h, _):
            m_copy(h).wait_send()
            l_copy(1, h).wait_send()
            l_copy(0, h).wait_send()
            return 0

        lax.fori_loop(0, nh, drain, 0)
        for i in range(3):
            lse_copy(i).wait_send()

    @pl.when(has_left)
    def _():
        for cp in id_left:
            cp.wait_send()

        @pl.when(core == 1)
        def _():
            for g in range(ng):
                for kk in range(2):
                    qg_copy(g, kk).wait_send()

        @pl.when(core == 0)
        def _():
            for g in range(ng):
                for kk in range(2):
                    qf_copy(0, g, kk).wait_send()
                    qf_copy(1, g, kk).wait_send()

    for p in puts:
        put(*p, sent)
    own_sum.wait()
    far_sum.wait_send()
    arrived(sum_ref.at[other], sum_rs)
    for slot, side, start, size, g, heads in puts:

        @pl.when(core == side)
        def _():
            to = pl.ds(pl.multiple_of(other * w + g * heads * D, D), heads * D)
            arrived(out_ref.at[pl.ds(start, size), to], oo_rs.at[slot])


CHUNKS = 8


def finish(nh, out_in, sum_in, out_ref, sum_ref, sem):
    size = out_in.shape[0] // CHUNKS
    cps = [
        pltpu.make_async_copy(
            out_in.at[pl.ds(i * size, size), :], out_ref.at[pl.ds(i * size, size), :], sem.at[i]
        )
        for i in range(CHUNKS)
    ]
    for cp in cps:
        cp.start()
    for i in range(2):
        sum_ref[pl.ds(i * nh, nh), :] = sum_in[i, pl.ds(0, nh), :]
    for cp in cps:
        cp.wait()


def shards(mesh, queries, keys, values, segment_ids):
    n, ncp = mesh.size, mesh.shape["cp"]
    width = queries.shape[1]
    heads = width // D
    nh = heads // 2
    ng, no = nh // QG, nh // OG
    w = nh * D
    pad = -(-nh // 8) * 8
    dma = pltpu.SemaphoreType.DMA
    scratch = [
        pltpu.VMEM((6, 1, T), jnp.int32),
        pltpu.VMEM((2 * T, w), BF16),
        pltpu.VMEM((2 * T, w), BF16),
        pltpu.VMEM((2 * T, w), BF16),
        pltpu.VMEM((T, w), BF16),
        pltpu.VMEM((T, w), BF16),
        pltpu.VMEM((PART, w), BF16),
        pltpu.VMEM((PART, w), BF16),
        pltpu.VMEM((nh, T, D), BF16),
        pltpu.VMEM((nh, T, D), BF16),
        pltpu.VMEM((2, nh, HALF, D), BF16),
        pltpu.VMEM((2, nh, HALF, D), BF16),
        pltpu.VMEM((3, pad, T), F32),
        pltpu.VMEM((3, pad, T), F32),
        pltpu.VMEM((T, 2 * T), F32),
        pltpu.VMEM((T, 3 * T), F32),
        pltpu.VMEM((2 * T, 2 * T), F32),
        pltpu.VMEM((2 * T, T), F32),
        pltpu.VMEM((nh, 2 * T, 2 * D), F32),
        pltpu.VMEM((nh, 2 * T, D), F32),
        pltpu.VMEM((nh, 2 * T, D), F32),
        pltpu.VMEM((nh, 2 * T, D), F32),
        pltpu.VMEM((2, T, w), BF16),
        pltpu.VMEM((2, pad, T), F32),
        pltpu.SemaphoreType.REGULAR,
        dma((5,)),
        dma((6,)),
        dma((4,)),
        dma((3,)),
        dma((3,)),
        dma((2, 2)),
        dma((2,)),
        dma((2, ng)),
        dma((ng,)),
        dma((2, 2, ng)),
        dma((2, ng)),
        dma((nh,)),
        dma((nh,)),
        dma((2, nh)),
        dma((2, nh)),
        dma((3,)),
        dma((3,)),
        dma((2 + no,)),
        dma((2 + no,)),
        dma((2,)),
        dma,
    ]
    anywhere = pl.BlockSpec(memory_space=pl.ANY)
    vmem = pl.BlockSpec(memory_space=pltpu.VMEM)
    out, sums = pl.pallas_call(
        functools.partial(kernel, n, ncp, nh),
        out_shape=(
            jax.ShapeDtypeStruct((T, width), BF16),
            jax.ShapeDtypeStruct((2, pad, T), F32),
        ),
        in_specs=[anywhere, anywhere, anywhere, anywhere],
        out_specs=(anywhere, anywhere),
        scratch_shapes=scratch,
        compiler_params=pltpu.CompilerParams(
            collective_id=0, has_side_effects=True, vmem_limit_bytes=53 * 2**20
        ),
        cost_estimate=pl.CostEstimate(
            flops=heads * T * T * D * 20, bytes_accessed=8 * T * width, transcendentals=0
        ),
    )(queries, keys, values, segment_ids.reshape(1, T))
    return pl.pallas_call(
        functools.partial(finish, nh),
        out_shape=(
            jax.ShapeDtypeStruct((T, width), BF16),
            jax.ShapeDtypeStruct((heads, T), F32),
        ),
        in_specs=[anywhere, vmem],
        out_specs=(anywhere, vmem),
        scratch_shapes=[dma((CHUNKS,))],
        compiler_params=pltpu.CompilerParams(vmem_limit_bytes=48 * 2**20),
    )(out, sums)


def solution(mesh):
    both = ("grp", "cp")
    return jax.shard_map(
        functools.partial(shards, mesh),
        mesh=mesh,
        in_specs=(P(both, None), P(both, None), P(both, None), P(both)),
        out_specs=(P(both, None), P(None, both)),
        check_vma=False,
    )
```

time: 53.1 us -> 49.1 us (0.925)
  the two profiles are of different devices: /device:TPU:1 before, /device:TPU:6 now
where the time goes in v2:
time: 49.1 us; the launch traced here: 48.7 us
  Pallas kernels  47.4 us (97%)
  local copies, waits for them, and re-layouts  0.65 us (1%)
  between operations  0.65 us (1%)
    pallas_call x1, Pallas kernels, shards(): pl.pallas_call(functools.partial(kernel, n, ncp, nh), out_shape=(jax.Shap...  45.8 us
    pallas_call x1, Pallas kernels, shards(): pl.pallas_call(functools.partial(finish, nh), out_shape=(jax.ShapeDtypeSt...  1.54 us

profile of v2, /device:TPU:6, one launch (start us, length us, event | category | flops | bytes accessed | tf_op | source)
XLA Modules:
  0.0 48.7 jit_solution(2550791140189306090)
XLA Ops:
  0.6 0.0 copy-start
  0.6 0.6 %copy-done = s32[128]{0:T(128)S(1)} copy-done((s32[128]{0:T(128)S(1)}, s32[128]{0:T(128)}, u32[]{:S(2)}) %copy-start) | copy-done | bytes 536
  1.3 45.8 %shard_map.59 = (bf16[128,3072]{1,0:T(8,128)(2,1)S(1)}, f32[2,16,128]{2,1,0:T(8,128)S(1)}) custom-call(bf16[128,3072]{1,0:T(8,128)(2,1)} %q_ref.1, bf16[128,3072]{1,0:T(8,128)(2,1)} %k_ref.1, bf16[128,3072]{1,0:T(8,128)(2,1)} %v_ref.1, s32[1,128]{1,0:T(1,128)S(1)} %bitcast.1), custom_call_target="tpu_custom_call" | custom-call | flops 1006632960 | bytes 3145728 | tf_op jit(solution)/shard_map/pallas_call | solution.py:660
  47.1 1.5 %shard_map.60 = (bf16[128,3072]{1,0:T(8,128)(2,1)}, f32[24,128]{1,0:T(8,128)}) custom-call(bf16[128,3072]{1,0:T(8,128)(2,1)S(1)} %get-tuple-element.4.out_in, f32[2,16,128]{2,1,0:T(8,128)S(1)} %get-tuple-element.5.sum_in), custom_call_target="tpu_custom_call" | custom-call | tf_op jit(solution)/shard_map/pallas_call | solution.py:676
Async XLA Ops:
  0.6 0.7 %copy-start = (s32[128]{0:T(128)S(1)}, s32[128]{0:T(128)}, u32[]{:S(2)}) copy-start(s32[128]{0:T(128)} %param.7) | copy-start | bytes 1540

commit v3 on v2

v3 whole, which is shorter than its diff:
```python
import functools
import math

import jax
import jax.numpy as jnp
from jax import lax
from jax.experimental import pallas as pl
from jax.experimental.pallas import tpu as pltpu
from jax.sharding import PartitionSpec as P

T = 128
HALF = T // 2
PART = T // 4
G = 96
MID = G // 2
END = T - PART - MID
D = 128
HIDDEN = -1e30
C2 = 1.0 / math.sqrt(D) / math.log(2.0)
LN2 = math.log(2.0)
MESH = pl.DeviceIdType.MESH
F32 = jnp.float32
BF16 = jnp.bfloat16

QG = 2
OG = 4
LINE = 16
AHEAD = 6
TWO = 2
PUMP = 12
MORE = 2
LINE = 16


def wide(h):
    return pl.ds(pl.multiple_of(h * D, D), D)


def scores(q, k, bias):
    return lax.dot_general(q, k, (((1,), (1,)), ((), ())), preferred_element_type=F32) + bias


def weigh(p, v):
    return lax.dot_general(
        p.astype(BF16), v, (((1,), (0,)), ((), ())), preferred_element_type=F32
    )


def attend(q, k, v, bias):
    s = scores(q, k, bias)
    top = jnp.max(s, axis=1, keepdims=True)
    p = jnp.exp2((s - top) * C2)
    total = jnp.sum(p, axis=1, keepdims=True)
    return weigh(p, v) * (1.0 / total), top * C2 + jnp.log2(total)


def kernel(
    n,
    ncp,
    nh,
    q_ref,
    k_ref,
    v_ref,
    id_ref,
    out_ref,
    sum_ref,
    ids,
    q2,
    k2,
    v2,
    qg,
    qf,
    ek,
    ev,
    m_send,
    m_recv,
    l_send,
    l_recv,
    lse_send,
    lse_recv,
    bias_g,
    bias_f,
    bias_o,
    bias_a,
    o_loc,
    s_loc,
    stage,
    sums,
    go,
    id_ss,
    id_rs,
    lo_s,
    sib_ss,
    sib_rs,
    e_ss,
    e_rs,
    q_ss,
    q_rs,
    m_ss,
    m_rs,
    l_ss,
    l_rs,
    lse_ss,
    lse_rs,
    oo_ss,
    oo_rs,
    sum_ss,
    sum_rs,
):
    w = nh * D
    ng = nh // QG
    no = nh // OG
    me = lax.axis_index("grp") * ncp + lax.axis_index("cp")
    core = lax.rem(me, 2)
    first = me - core
    other = 1 - core
    has_left = first > 0
    has_right = first < n - 2
    waits = lax.rem(first, LINE) == 0
    prompt = jnp.logical_not(waits)
    ends = lax.rem(first, LINE) == LINE - 2

    def at(i):
        i = lax.rem(i + n, n)
        return (i // ncp, lax.rem(i, ncp))

    sib = at(first + other)
    right = [at(first + 2), at(first + 3)]
    left = [at(first - 2), at(first - 1)]
    ahead = at(me + 2)
    behind_me = at(me - 2)

    def remote(src, dst, ss, rs, to):
        return pltpu.make_async_remote_copy(
            src_ref=src, dst_ref=dst, send_sem=ss, recv_sem=rs, device_id=to, device_id_type=MESH
        )

    def greet(sem, to):
        pl.semaphore_signal(sem, inc=1, device_id=to, device_id_type=MESH)

    def arrived(dst, rs):
        remote(dst, dst, sum_ss.at[0], rs, sib).wait_recv()

    barrier = pltpu.get_barrier_semaphore()
    greet(barrier, sib)

    @pl.when(has_left)
    def _():
        greet(barrier, left[0])
        greet(barrier, left[1])

    mine = pl.ds(pl.multiple_of(core * w, D), w)
    its = pl.ds(pl.multiple_of(other * w, D), w)
    my_rows = pl.ds(pl.multiple_of(core * T, T), T)
    its_rows = pl.ds(pl.multiple_of(other * T, T), T)
    trio = ((k_ref, k2), (v_ref, v2), (q_ref, q2))
    local = [
        pltpu.make_async_copy(a.at[:, mine], b.at[my_rows, :], lo_s.at[i])
        for i, (a, b) in enumerate(trio)
    ]
    local.append(pltpu.make_async_copy(id_ref, ids.at[2 + core], lo_s.at[3]))
    for cp in local:
        cp.start()
    pl.semaphore_wait(barrier, 1 + 2 * has_right.astype(jnp.int32))

    @pl.when(has_right)
    def _():
        greet(go, right[0])
        greet(go, right[1])

    id_sib = remote(id_ref, ids.at[2 + core], id_ss.at[0], id_rs.at[2 + core], sib)
    id_right = [
        remote(id_ref, ids.at[core], id_ss.at[1 + i], id_rs.at[core], right[i]) for i in range(2)
    ]
    id_left = [
        remote(id_ref, ids.at[4 + core], id_ss.at[3 + i], id_rs.at[4 + core], left[i])
        for i in range(2)
    ]
    sib_sends = [
        remote(a.at[:, its], b.at[my_rows, :], sib_ss.at[i], sib_rs.at[i], sib)
        for i, (a, b) in enumerate(trio)
    ]

    def e_copy(i):
        a, b = ((k2, ek), (v2, ev))[i]
        return remote(a.at[pl.ds(2 * T - END, END), :], b, e_ss.at[i], e_rs.at[i], ahead)

    def q_cols(g):
        return pl.ds(pl.multiple_of(g * QG * D, D), QG * D)

    pieces = ((T, qg, 0, G), (HALF, qf, HALF, HALF), (0, qf, 0, HALF))

    def q_copy(piece, g):
        start, to, row, size = pieces[piece]
        return remote(
            q2.at[pl.ds(start, size), q_cols(g)],
            to.at[pl.ds(row, size), q_cols(g)],
            q_ss.at[piece, g],
            q_rs.at[piece, g],
            behind_me,
        )

    def q_arrived(piece, g):
        _, to, row, size = pieces[piece]
        arrived(to.at[pl.ds(row, size), q_cols(g)], q_rs.at[piece, g])

    def q_next(i):
        for piece in range(3):

            @pl.when(has_left & (i >= piece * ng) & (i < (piece + 1) * ng))
            def _():
                q_copy(piece, i - piece * ng).start()

    sib_sends[2].start()
    id_sib.start()
    sib_sends[0].start()
    sib_sends[1].start()

    @pl.when(has_right)
    def _():
        id_right[0].start()
        id_right[1].start()

    @pl.when(jnp.logical_not(has_left))
    def _():
        ids[0] = jnp.full((1, T), -1, jnp.int32)
        ids[1] = jnp.full((1, T), -1, jnp.int32)
        ek[...] = jnp.zeros(ek.shape, BF16)
        ev[...] = jnp.zeros(ev.shape, BF16)
        m_recv[...] = jnp.zeros(m_recv.shape, BF16)
        l_recv[...] = jnp.zeros(l_recv.shape, BF16)
        lse_recv[...] = jnp.full(lse_recv.shape, HIDDEN, F32)

    @pl.when(jnp.logical_not(has_right))
    def _():
        ids[4] = jnp.full((1, T), -2, jnp.int32)
        ids[5] = jnp.full((1, T), -2, jnp.int32)

    def iota(shape, axis):
        return lax.broadcasted_iota(jnp.int32, shape, axis)

    eye = iota((T, T), 0) == iota((T, T), 1)
    eyes = [iota((HALF, T), 0) + HALF * i == iota((HALF, T), 1) for i in range(2)]
    eye_g = iota((G, T), 0) == iota((G, T), 1)

    def to_column(r, like):
        return jnp.sum(
            jnp.where(like, jnp.broadcast_to(r, like.shape), 0.0), axis=1, keepdims=True
        )

    def to_row(x, like):
        return jnp.sum(jnp.where(like, x, 0.0), axis=0, keepdims=True)

    def bias_of(q_col, k_row):
        return jnp.where(q_col == k_row, 0.0, HIDDEN)

    def have(i):
        local[i].wait()
        arrived(trio[i][1].at[its_rows, :], sib_rs.at[i])

    have(0)
    have(1)

    @pl.when(has_right)
    def _():
        e_copy(0).start()
        e_copy(1).start()

    have(2)
    arrived(ids.at[2 + other], id_rs.at[2 + other])
    local[3].wait()
    own = [ids[2].astype(F32), ids[3].astype(F32)]
    own_col = [to_column(r, eye) for r in own]
    for i in range(2):
        for j in range(2):
            bias_o[pl.ds(i * T, T), pl.ds((j + 1) * T, T)] = (
                bias_of(own_col[i], own[j]) if j <= i else jnp.full((T, T), HIDDEN, F32)
            )

    lane = iota((1, T), 1)

    def short(a, b):
        edge = jnp.sum(jnp.where(lane == T - PART - 1, a, 0.0), axis=1, keepdims=True)
        return edge != jnp.max(b, axis=1, keepdims=True)

    kv_row = jnp.broadcast_to(jnp.where(short(*own), 1.0, 0.0), (1, D))

    @pl.when(has_left)
    def _():
        pl.semaphore_wait(go, 2)
        id_left[0].start()
        id_left[1].start()
        for i in range(AHEAD):

            @pl.when(prompt | (i < TWO))
            def _():
                q_copy(i // ng, i % ng).start()

    @pl.when(has_right)
    def _():
        arrived(ids.at[4], id_rs.at[4])
        arrived(ids.at[5], id_rs.at[5])

    its_col = [to_column(ids[4 + i].astype(F32), eye) for i in range(2)]
    for j in range(2):
        bias_g[:, pl.ds(j * T, T)] = bias_of(its_col[1][:G], own[j])
        bias_f[:, pl.ds((j + 1) * T, T)] = bias_of(its_col[0], own[j])

    def m_copy(h):
        return remote(m_send.at[h], m_recv.at[h], m_ss.at[h], m_rs.at[h], ahead)

    def l_copy(part, h):
        return remote(
            l_send.at[part, h], l_recv.at[part, h], l_ss.at[part, h], l_rs.at[part, h], ahead
        )

    def lse_copy(i, g):
        return remote(
            lse_send.at[i, g], lse_recv.at[i, g], lse_ss.at[i, g], lse_rs.at[i, g], ahead
        )

    def step_g(g, _):
        @pl.when(prompt)
        def _():
            q_next(AHEAD + g)

        @pl.when(waits & has_left)
        def _():
            q_copy(0, g).wait_send()
            q_next(TWO + g)

        @pl.when(has_right)
        def _():
            q_arrived(0, g)

        kv = kv_row > 0.5
        for u in range(QG):
            h = g * QG + u
            o, lse = attend(qg[:, wide(h)], k2[:, wide(h)], v2[:, wide(h)], bias_g[...])
            lse_send[0, g, pl.ds(u, 1), :] = jnp.where(kv | (lane >= G), HIDDEN, to_row(lse, eye_g))
            rows = pl.ds(T + PART, MID)
            there = jnp.concatenate([k2[rows, wide(h)], v2[rows, wide(h)]], axis=0)
            m_send[h] = jnp.where(kv, there.astype(F32), o).astype(BF16)

            @pl.when(has_right)
            def _():
                m_copy(h).start()

        @pl.when(has_right)
        def _():
            lse_copy(0, g).start()

        return 0

    lax.fori_loop(0, ng, step_g, 0)

    @pl.when(waits & has_left)
    def _():
        for i in range(TWO + ng, PUMP):
            q_copy((i - TWO) // ng, (i - TWO) % ng).wait_send()
            q_copy(i // ng, i % ng).start()

    @pl.when(has_left)
    def _():
        arrived(ids.at[0], id_rs.at[0])
        arrived(ids.at[1], id_rs.at[1])
        arrived(ek, e_rs.at[0])
        arrived(ev, e_rs.at[1])

    before = [ids[i].astype(F32) for i in range(2)]
    seen = [jnp.where(short(*before), r, -1.0) for r in before]
    behind = seen[1]
    low_keys = jnp.concatenate([seen[0][:, T - PART :], behind[:, :PART]], axis=1)
    for i in range(2):
        rows = pl.ds(i * T, T)
        bias_o[rows, pl.ds(0, T)] = jnp.where(
            iota((T, T), 1) < PART, HIDDEN, bias_of(own_col[i], behind)
        )
        bias_a[rows, :] = bias_of(own_col[i], low_keys)
    late = (iota((T, T), 0) >= HALF) & (iota((T, T), 1) < PART)
    bias_f[:, pl.ds(0, T)] = jnp.where(late, HIDDEN, bias_of(its_col[0], behind))

    def near(h):
        none = jnp.zeros((PART, D), BF16)
        got = m_recv[h]
        keys = jnp.concatenate([none, got[:MID], ek[:, wide(h)], k2[:, wide(h)]], axis=0)
        vals = jnp.concatenate([none, got[MID:], ev[:, wide(h)], v2[:, wide(h)]], axis=0)
        return keys, vals

    def own(h, keys, vals):
        o_loc[h], lse = attend(q2[:, wide(h)], keys, vals, bias_o[...])
        s_loc[h] = jnp.broadcast_to(lse, (2 * T, D))

    def step_f1(g, _):
        @pl.when(waits)
        def _():
            for i in range(MORE):
                q_next(PUMP + g * MORE + i)

        @pl.when(prompt)
        def _():
            q_next(AHEAD + ng + g)

        @pl.when(has_right)
        def _():
            q_arrived(1, g)

        @pl.when(has_left)
        def _():
            for u in range(QG):
                arrived(m_recv.at[g * QG + u], m_rs.at[g * QG + u])

        def reply(u, o, lse):
            h = g * QG + u
            kv = kv_row > 0.5
            lse_send[1, g, pl.ds(u, 1), :] = jnp.where(
                kv | (lane < HALF), HIDDEN, to_row(lse, eyes[1])
            )
            rows = pl.ds(T, PART)
            there = jnp.concatenate([k2[rows, wide(h)], v2[rows, wide(h)]], axis=0)
            l_send[1, h] = jnp.where(kv, there.astype(F32), o).astype(BF16)

            @pl.when(has_right)
            def _():
                l_copy(1, h).start()

        @pl.when(jnp.logical_not(ends))
        def _():
            for u in range(QG):
                h = g * QG + u
                q = jnp.concatenate([qf[pl.ds(HALF, HALF), wide(h)], q2[:, wide(h)]], axis=0)
                bias = jnp.concatenate([bias_f[pl.ds(HALF, HALF), :], bias_o[...]], axis=0)
                o, lse = attend(q, *near(h), bias)
                reply(u, o[:HALF], lse[:HALF])
                o_loc[h] = o[HALF:]
                s_loc[h] = jnp.broadcast_to(lse[HALF:], (2 * T, D))

        @pl.when(ends)
        def _():
            for u in range(QG):
                h = g * QG + u
                q, bias = qf[pl.ds(HALF, HALF), wide(h)], bias_f[pl.ds(HALF, HALF), :]
                reply(u, *attend(q, *near(h), bias))

        @pl.when(has_right)
        def _():
            lse_copy(1, g).start()

        return 0

    lax.fori_loop(0, ng, step_f1, 0)

    def step_f0(g, _):
        @pl.when(prompt)
        def _():
            q_next(AHEAD + 2 * ng + g)

        @pl.when(has_right)
        def _():
            q_arrived(2, g)

        @pl.when(has_left)
        def _():
            for u in range(QG):
                arrived(l_recv.at[1, g * QG + u], l_rs.at[1, g * QG + u])

        kv = kv_row > 0.5
        for u in range(QG):
            h = g * QG + u
            low, got = l_recv[1, h], m_recv[h]
            keys = jnp.concatenate(
                [low[:PART], got[:MID], ek[:, wide(h)], k2[:, wide(h)]], axis=0
            )
            vals = jnp.concatenate(
                [low[PART:], got[MID:], ev[:, wide(h)], v2[:, wide(h)]], axis=0
            )
            o, lse = attend(qf[pl.ds(0, HALF), wide(h)], keys, vals, bias_f[pl.ds(0, HALF), :])
            lse_send[2, g, pl.ds(u, 1), :] = jnp.where(
                kv | (lane >= HALF), HIDDEN, to_row(lse, eyes[0])
            )
            rows = pl.ds(T - PART, PART)
            there = jnp.concatenate([k2[rows, wide(h)], v2[rows, wide(h)]], axis=0)
            l_send[0, h] = jnp.where(kv, there.astype(F32), o).astype(BF16)

            @pl.when(has_right)
            def _():
                l_copy(0, h).start()

        @pl.when(has_right)
        def _():
            lse_copy(2, g).start()

        return 0

    lax.fori_loop(0, ng, step_f0, 0)

    @pl.when(ends)
    def _():
        def step_own(g, _):
            for u in range(QG):
                own(g * QG + u, *near(g * QG + u))
            return 0

        lax.fori_loop(0, ng, step_own, 0)

    def put(g, side, act):
        cols = pl.ds(g * OG * D, OG * D)
        to = pl.ds(pl.multiple_of(core * w + g * OG * D, D), OG * D)
        src, dst, sem = stage.at[side, :, cols], out_ref.at[:, to], oo_ss.at[side, g]

        @pl.when(core == side)
        def _():
            act(pltpu.make_async_copy(src, dst, sem), False)

        @pl.when(core != side)
        def _():
            act(remote(src, dst, sem, oo_rs.at[g], sib), True)

    def begin(cp, far):
        cp.start()

    def sent(cp, far):
        if far:
            cp.wait_send()
        else:
            cp.wait()

    @pl.when(has_left)
    def _():
        for i in range(2):
            for g in range(ng):
                arrived(lse_recv.at[i, g], lse_rs.at[i, g])

    def finish_heads(i, g):
        step = g * (OG // QG) + i

        @pl.when(has_left)
        def _():
            arrived(lse_recv.at[2, step], lse_rs.at[2, step])
            for u in range(QG):
                h = step * QG + u
                arrived(l_recv.at[0, h], l_rs.at[0, h])

        for u in range(QG):
            h = step * QG + u
            low, mid = l_recv[0, h], l_recv[1, h]
            keys = jnp.concatenate([low[:PART], mid[:PART]], axis=0)
            vals = jnp.concatenate([low[PART:], mid[PART:]], axis=0)
            theirs = jnp.concatenate([low, mid, m_recv[h], jnp.zeros((T - G, D), BF16)], axis=0)
            f_lse = jnp.maximum(
                lse_recv[1, step, pl.ds(u, 1), :], lse_recv[2, step, pl.ds(u, 1), :]
            )
            there = jnp.concatenate(
                [to_column(f_lse, eye), to_column(lse_recv[0, step, pl.ds(u, 1), :], eye)], axis=0
            )
            here = s_loc[h]
            s = scores(q2[:, wide(h)], keys, bias_a[...]) * C2
            top = jnp.maximum(jnp.max(s, axis=1, keepdims=True), there)
            top = jnp.maximum(here, top)
            p = jnp.exp2(s - top[:, :HALF])
            fade = jnp.exp2(here - top)
            extra = jnp.exp2(there - top)
            total = fade + extra + jnp.sum(p, axis=1, keepdims=True)
            out = o_loc[h] * fade + weigh(p, vals) + theirs.astype(F32) * extra
            out = (out / total).astype(BF16)
            lse = (top + jnp.log2(total)) * LN2
            for side in range(2):
                rows = slice(side * T, side * T + T)
                stage[side, :, wide(h)] = out[rows]
                sums[side, pl.ds(h, 1), :] = to_row(lse[rows], eye)
        return g

    for g in range(no):
        lax.fori_loop(0, OG // QG, finish_heads, g)
        put(g, 0, begin)
        put(g, 1, begin)

    own_sum = pltpu.make_async_copy(sums.at[core], sum_ref.at[core], sum_ss.at[0])
    far_sum = remote(sums.at[other], sum_ref.at[core], sum_ss.at[1], sum_rs, sib)
    own_sum.start()
    far_sum.start()

    id_sib.wait_send()
    for cp in sib_sends:
        cp.wait_send()

    @pl.when(has_right)
    def _():
        for cp in id_right:
            cp.wait_send()

        e_copy(0).wait_send()
        e_copy(1).wait_send()

        def drain(h, _):
            m_copy(h).wait_send()
            l_copy(1, h).wait_send()
            l_copy(0, h).wait_send()
            return 0

        lax.fori_loop(0, nh, drain, 0)
        for i in range(3):
            for g in range(ng):
                lse_copy(i, g).wait_send()

    @pl.when(has_left)
    def _():
        for cp in id_left:
            cp.wait_send()
        for i in range(3 * ng):

            @pl.when(prompt | (i >= PUMP - TWO))
            def _():
                q_copy(i // ng, i % ng).wait_send()

    for g in range(no):
        put(g, 0, sent)
        put(g, 1, sent)
        to = pl.ds(pl.multiple_of(other * w + g * OG * D, D), OG * D)
        arrived(out_ref.at[:, to], oo_rs.at[g])
    own_sum.wait()
    far_sum.wait_send()
    arrived(sum_ref.at[other], sum_rs)


CHUNKS = 8


def finish(nh, out_in, sum_in, out_ref, sum_ref, sem):
    size = out_in.shape[0] // CHUNKS
    cps = [
        pltpu.make_async_copy(
            out_in.at[pl.ds(i * size, size), :], out_ref.at[pl.ds(i * size, size), :], sem.at[i]
        )
        for i in range(CHUNKS)
    ]
    for cp in cps:
        cp.start()
    for i in range(2):
        sum_ref[pl.ds(i * nh, nh), :] = sum_in[i, pl.ds(0, nh), :]
    for cp in cps:
        cp.wait()


def shards(mesh, queries, keys, values, segment_ids):
    n, ncp = mesh.size, mesh.shape["cp"]
    width = queries.shape[1]
    heads = width // D
    nh = heads // 2
    ng, no = nh // QG, nh // OG
    w = nh * D
    pad = -(-nh // 8) * 8
    dma = pltpu.SemaphoreType.DMA
    scratch = [
        pltpu.VMEM((6, 1, T), jnp.int32),
        pltpu.VMEM((2 * T, w), BF16),
        pltpu.VMEM((2 * T, w), BF16),
        pltpu.VMEM((2 * T, w), BF16),
        pltpu.VMEM((G, w), BF16),
        pltpu.VMEM((T, w), BF16),
        pltpu.VMEM((END, w), BF16),
        pltpu.VMEM((END, w), BF16),
        pltpu.VMEM((nh, G, D), BF16),
        pltpu.VMEM((nh, G, D), BF16),
        pltpu.VMEM((2, nh, HALF, D), BF16),
        pltpu.VMEM((2, nh, HALF, D), BF16),
        pltpu.VMEM((3, ng, 8, T), F32),
        pltpu.VMEM((3, ng, 8, T), F32),
        pltpu.VMEM((G, 2 * T), F32),
        pltpu.VMEM((T, 3 * T), F32),
        pltpu.VMEM((2 * T, 3 * T), F32),
        pltpu.VMEM((2 * T, HALF), F32),
        pltpu.VMEM((nh, 2 * T, D), F32),
        pltpu.VMEM((nh, 2 * T, D), F32),
        pltpu.VMEM((2, T, w), BF16),
        pltpu.VMEM((2, pad, T), F32),
        pltpu.SemaphoreType.REGULAR,
        dma((5,)),
        dma((6,)),
        dma((4,)),
        dma((3,)),
        dma((3,)),
        dma((2,)),
        dma((2,)),
        dma((3, ng)),
        dma((3, ng)),
        dma((nh,)),
        dma((nh,)),
        dma((2, nh)),
        dma((2, nh)),
        dma((3, ng)),
        dma((3, ng)),
        dma((2, no)),
        dma((no,)),
        dma((2,)),
        dma,
    ]
    anywhere = pl.BlockSpec(memory_space=pl.ANY)
    vmem = pl.BlockSpec(memory_space=pltpu.VMEM)
    out, sums = pl.pallas_call(
        functools.partial(kernel, n, ncp, nh),
        out_shape=(
            jax.ShapeDtypeStruct((T, width), BF16),
            jax.ShapeDtypeStruct((2, pad, T), F32),
        ),
        in_specs=[anywhere, anywhere, anywhere, anywhere],
        out_specs=(anywhere, anywhere),
        scratch_shapes=scratch,
        compiler_params=pltpu.CompilerParams(
            collective_id=0, has_side_effects=True, vmem_limit_bytes=53 * 2**20
        ),
        cost_estimate=pl.CostEstimate(
            flops=heads * T * T * D * 20, bytes_accessed=8 * T * width, transcendentals=0
        ),
    )(queries, keys, values, segment_ids.reshape(1, T))
    return pl.pallas_call(
        functools.partial(finish, nh),
        out_shape=(
            jax.ShapeDtypeStruct((T, width), BF16),
            jax.ShapeDtypeStruct((heads, T), F32),
        ),
        in_specs=[anywhere, vmem],
        out_specs=(anywhere, vmem),
        scratch_shapes=[dma((CHUNKS,))],
        compiler_params=pltpu.CompilerParams(vmem_limit_bytes=48 * 2**20),
    )(out, sums)


def solution(mesh):
    both = ("grp", "cp")
    return jax.shard_map(
        functools.partial(shards, mesh),
        mesh=mesh,
        in_specs=(P(both, None), P(both, None), P(both, None), P(both)),
        out_specs=(P(both, None), P(None, both)),
        check_vma=False,
    )
```

time: 49.1 us -> 42.9 us (0.87)
  Pallas kernels: 47.4 us -> 40.9 us
    pallas_call x1, Pallas kernels: 45.8 us -> 39.4 us  [shards(): pl.pallas_call(functools.partial(kernel, n, ncp, nh), out_shape=(jax.Shap...]
where the time goes in v3:
time: 42.9 us; the launch traced here: 42.2 us
  Pallas kernels  40.9 us (95%)
  local copies, waits for them, and re-layouts  0.65 us (2%)
  between operations  0.65 us (2%)
    pallas_call x1, Pallas kernels, shards(): pl.pallas_call(functools.partial(kernel, n, ncp, nh), out_shape=(jax.Shap...  39.4 us
    pallas_call x1, Pallas kernels, shards(): pl.pallas_call(functools.partial(finish, nh), out_shape=(jax.ShapeDtypeSt...  1.54 us

profile of v3, /device:TPU:6, one launch (start us, length us, event | category | flops | bytes accessed | tf_op | source)
XLA Modules:
  0.0 42.2 jit_solution(12947907657218143064)
XLA Ops:
  0.6 0.0 copy-start
  0.6 0.6 %copy-done = s32[128]{0:T(128)S(1)} copy-done((s32[128]{0:T(128)S(1)}, s32[128]{0:T(128)}, u32[]{:S(2)}) %copy-start) | copy-done | bytes 536
  1.3 39.4 %shard_map.59 = (bf16[128,3072]{1,0:T(8,128)(2,1)S(1)}, f32[2,16,128]{2,1,0:T(8,128)S(1)}) custom-call(bf16[128,3072]{1,0:T(8,128)(2,1)} %q_ref.1, bf16[128,3072]{1,0:T(8,128)(2,1)} %k_ref.1, bf16[128,3072]{1,0:T(8,128)(2,1)} %v_ref.1, s32[1,128]{1,0:T(1,128)S(1)} %bitcast.1), custom_call_target="tpu_custom_call" | custom-call | flops 1006632960 | bytes 3145728 | tf_op jit(solution)/shard_map/pallas_call | solution.py:700
  40.7 1.5 %shard_map.60 = (bf16[128,3072]{1,0:T(8,128)(2,1)}, f32[24,128]{1,0:T(8,128)}) custom-call(bf16[128,3072]{1,0:T(8,128)(2,1)S(1)} %get-tuple-element.4.out_in, f32[2,16,128]{2,1,0:T(8,128)S(1)} %get-tuple-element.5.sum_in), custom_call_target="tpu_custom_call" | custom-call | tf_op jit(solution)/shard_map/pallas_call | solution.py:716
Async XLA Ops:
  0.6 0.7 %copy-start = (s32[128]{0:T(128)S(1)}, s32[128]{0:T(128)}, u32[]{:S(2)}) copy-start(s32[128]{0:T(128)} %param.7) | copy-start | bytes 1540

commit v4 on v3

--- a/solution.py
+++ b/solution.py
@@ -27,7 +27,7 @@
 LINE = 16
 AHEAD = 6
 TWO = 2
-PUMP = 12
+PUMP = 18
 MORE = 2
 LINE = 16
 
@@ -78,10 +78,10 @@
     l_recv,
     lse_send,
     lse_recv,
-    bias_g,
-    bias_f,
+    bias_r,
     bias_o,
     bias_a,
+    for_me,
     o_loc,
     s_loc,
     stage,
@@ -119,6 +119,7 @@
     waits = lax.rem(first, LINE) == 0
     prompt = jnp.logical_not(waits)
     ends = lax.rem(first, LINE) == LINE - 2
+    lead = jnp.where(ends, PUMP, jnp.where(waits, TWO, AHEAD))
 
     def at(i):
         i = lax.rem(i + n, n)
@@ -172,29 +173,37 @@
     id_right = [
         remote(id_ref, ids.at[core], id_ss.at[1 + i], id_rs.at[core], right[i]) for i in range(2)
     ]
-    id_left = [
-        remote(id_ref, ids.at[4 + core], id_ss.at[3 + i], id_rs.at[4 + core], left[i])
-        for i in range(2)
-    ]
     sib_sends = [
         remote(a.at[:, its], b.at[my_rows, :], sib_ss.at[i], sib_rs.at[i], sib)
         for i, (a, b) in enumerate(trio)
     ]
 
-    def e_copy(i):
-        a, b = ((k2, ek), (v2, ev))[i]
-        return remote(a.at[pl.ds(2 * T - END, END), :], b, e_ss.at[i], e_rs.at[i], ahead)
+    def e_copies():
+        return [
+            remote(
+                a.at[pl.ds(T - END, END), pl.ds(kk * w, w)],
+                b,
+                e_ss.at[kk, i],
+                e_rs.at[i],
+                right[kk],
+            )
+            for kk in range(2)
+            for i, (a, b) in enumerate(((k_ref, ek), (v_ref, ev)))
+        ]
 
     def q_cols(g):
         return pl.ds(pl.multiple_of(g * QG * D, D), QG * D)
 
     pieces = ((T, qg, 0, G), (HALF, qf, HALF, HALF), (0, qf, 0, HALF))
+
+    def q_cut(piece, g):
+        return wide(g) if piece == 0 else q_cols(g)
 
     def q_copy(piece, g):
         start, to, row, size = pieces[piece]
         return remote(
-            q2.at[pl.ds(start, size), q_cols(g)],
-            to.at[pl.ds(row, size), q_cols(g)],
+            q2.at[pl.ds(start, size), q_cut(piece, g)],
+            to.at[pl.ds(row, size), q_cut(piece, g)],
             q_ss.at[piece, g],
             q_rs.at[piece, g],
             behind_me,
@@ -202,14 +211,16 @@
 
     def q_arrived(piece, g):
         _, to, row, size = pieces[piece]
-        arrived(to.at[pl.ds(row, size), q_cols(g)], q_rs.at[piece, g])
+        arrived(to.at[pl.ds(row, size), q_cut(piece, g)], q_rs.at[piece, g])
+
+    q_order = [(0, h) for h in range(nh)] + [(p, g) for p in (1, 2) for g in range(ng)]
 
     def q_next(i):
-        for piece in range(3):
-
-            @pl.when(has_left & (i >= piece * ng) & (i < (piece + 1) * ng))
+        for piece, start, count in ((0, 0, nh), (1, nh, ng), (2, nh + ng, ng)):
+
+            @pl.when(has_left & (i >= start) & (i < start + count))
             def _():
-                q_copy(piece, i - piece * ng).start()
+                q_copy(piece, i - start).start()
 
     sib_sends[2].start()
     id_sib.start()
@@ -220,6 +231,11 @@
     def _():
         id_right[0].start()
         id_right[1].start()
+
+        @pl.when(core == 1)
+        def _():
+            for cp in e_copies():
+                cp.start()
 
     @pl.when(jnp.logical_not(has_left))
     def _():
@@ -231,11 +247,6 @@
         l_recv[...] = jnp.zeros(l_recv.shape, BF16)
         lse_recv[...] = jnp.full(lse_recv.shape, HIDDEN, F32)
 
-    @pl.when(jnp.logical_not(has_right))
-    def _():
-        ids[4] = jnp.full((1, T), -2, jnp.int32)
-        ids[5] = jnp.full((1, T), -2, jnp.int32)
-
     def iota(shape, axis):
         return lax.broadcasted_iota(jnp.int32, shape, axis)
 
@@ -260,11 +271,6 @@
 
     have(0)
     have(1)
-
-    @pl.when(has_right)
-    def _():
-        e_copy(0).start()
-        e_copy(1).start()
 
     have(2)
     arrived(ids.at[2 + other], id_rs.at[2 + other])
@@ -288,23 +294,20 @@
     @pl.when(has_left)
     def _():
         pl.semaphore_wait(go, 2)
-        id_left[0].start()
-        id_left[1].start()
-        for i in range(AHEAD):
-
-            @pl.when(prompt | (i < TWO))
+        for i in range(PUMP):
+
+            @pl.when(i < lead)
             def _():
-                q_copy(i // ng, i % ng).start()
-
-    @pl.when(has_right)
-    def _():
-        arrived(ids.at[4], id_rs.at[4])
-        arrived(ids.at[5], id_rs.at[5])
-
-    its_col = [to_column(ids[4 + i].astype(F32), eye) for i in range(2)]
+                q_copy(*q_order[i]).start()
+
+    across = jnp.max(own[1], axis=1, keepdims=True)
+
+    def bias_across(k_row):
+        return jnp.where(k_row == across, 0.0, HIDDEN)
+
     for j in range(2):
-        bias_g[:, pl.ds(j * T, T)] = bias_of(its_col[1][:G], own[j])
-        bias_f[:, pl.ds((j + 1) * T, T)] = bias_of(its_col[0], own[j])
+        for i in range(2):
+            bias_r[pl.ds(i, 1), pl.ds((j + 1) * T, T)] = bias_across(own[j])
 
     def m_copy(h):
         return remote(m_send.at[h], m_recv.at[h], m_ss.at[h], m_rs.at[h], ahead)
@@ -319,46 +322,39 @@
             lse_send.at[i, g], lse_recv.at[i, g], lse_ss.at[i, g], lse_rs.at[i, g], ahead
         )
 
-    def step_g(g, _):
-        @pl.when(prompt)
-        def _():
-            q_next(AHEAD + g)
-
-        @pl.when(waits & has_left)
-        def _():
-            q_copy(0, g).wait_send()
-            q_next(TWO + g)
+    def step_g(h, _):
+        q_next(lead + h)
 
         @pl.when(has_right)
         def _():
-            q_arrived(0, g)
+            q_arrived(0, h)
 
         kv = kv_row > 0.5
-        for u in range(QG):
-            h = g * QG + u
-            o, lse = attend(qg[:, wide(h)], k2[:, wide(h)], v2[:, wide(h)], bias_g[...])
-            lse_send[0, g, pl.ds(u, 1), :] = jnp.where(kv | (lane >= G), HIDDEN, to_row(lse, eye_g))
-            rows = pl.ds(T + PART, MID)
-            there = jnp.concatenate([k2[rows, wide(h)], v2[rows, wide(h)]], axis=0)
-            m_send[h] = jnp.where(kv, there.astype(F32), o).astype(BF16)
-
-            @pl.when(has_right)
+        g, u = h // QG, lax.rem(h, QG)
+        o, lse = attend(
+            qg[:, wide(h)], k2[:, wide(h)], v2[:, wide(h)], bias_r[pl.ds(0, 1), pl.ds(T, 2 * T)]
+        )
+        lse_send[0, g, pl.ds(u, 1), :] = jnp.where(kv | (lane >= G), HIDDEN, to_row(lse, eye_g))
+        rows = pl.ds(T + PART, MID)
+        there = jnp.concatenate([k2[rows, wide(h)], v2[rows, wide(h)]], axis=0)
+        m_send[h] = jnp.where(kv, there.astype(F32), o).astype(BF16)
+
+        @pl.when(has_right)
+        def _():
+            m_copy(h).start()
+
+            @pl.when(u == QG - 1)
             def _():
-                m_copy(h).start()
-
-        @pl.when(has_right)
-        def _():
-            lse_copy(0, g).start()
+                lse_copy(0, g).start()
 
         return 0
 
-    lax.fori_loop(0, ng, step_g, 0)
+    lax.fori_loop(0, nh, step_g, 0)
 
     @pl.when(waits & has_left)
     def _():
-        for i in range(TWO + ng, PUMP):
-            q_copy((i - TWO) // ng, (i - TWO) % ng).wait_send()
-            q_copy(i // ng, i % ng).start()
+        for i in range(TWO + nh, PUMP):
+            q_copy(*q_order[i]).start()
 
     @pl.when(has_left)
     def _():
@@ -377,8 +373,11 @@
             iota((T, T), 1) < PART, HIDDEN, bias_of(own_col[i], behind)
         )
         bias_a[rows, :] = bias_of(own_col[i], low_keys)
-    late = (iota((T, T), 0) >= HALF) & (iota((T, T), 1) < PART)
-    bias_f[:, pl.ds(0, T)] = jnp.where(late, HIDDEN, bias_of(its_col[0], behind))
+    bias_r[pl.ds(0, 1), pl.ds(0, T)] = jnp.where(lane < PART, HIDDEN, bias_across(behind))
+    bias_r[pl.ds(1, 1), pl.ds(0, T)] = bias_across(behind)
+    from_left = jnp.max(before[1], axis=1, keepdims=True)
+    for i in range(2):
+        for_me[pl.ds(i, 1), :] = jnp.where(own[i] == from_left, 0.0, 2.0 * HIDDEN)
 
     def near(h):
         none = jnp.zeros((PART, D), BF16)
@@ -399,7 +398,7 @@
 
         @pl.when(prompt)
         def _():
-            q_next(AHEAD + ng + g)
+            q_next(lead + nh + g)
 
         @pl.when(has_right)
         def _():
@@ -429,7 +428,9 @@
             for u in range(QG):
                 h = g * QG + u
                 q = jnp.concatenate([qf[pl.ds(HALF, HALF), wide(h)], q2[:, wide(h)]], axis=0)
-                bias = jnp.concatenate([bias_f[pl.ds(HALF, HALF), :], bias_o[...]], axis=0)
+                bias = jnp.concatenate(
+                    [jnp.broadcast_to(bias_r[pl.ds(0, 1), :], (HALF, 3 * T)), bias_o[...]], axis=0
+                )
                 o, lse = attend(q, *near(h), bias)
                 reply(u, o[:HALF], lse[:HALF])
                 o_loc[h] = o[HALF:]
@@ -439,7 +440,7 @@
         def _():
             for u in range(QG):
                 h = g * QG + u
-                q, bias = qf[pl.ds(HALF, HALF), wide(h)], bias_f[pl.ds(HALF, HALF), :]
+                q, bias = qf[pl.ds(HALF, HALF), wide(h)], bias_r[pl.ds(0, 1), :]
                 reply(u, *attend(q, *near(h), bias))
 
         @pl.when(has_right)
@@ -453,7 +454,7 @@
     def step_f0(g, _):
         @pl.when(prompt)
         def _():
-            q_next(AHEAD + 2 * ng + g)
+            q_next(lead + nh + ng + g)
 
         @pl.when(has_right)
         def _():
@@ -474,7 +475,7 @@
             vals = jnp.concatenate(
                 [low[PART:], got[MID:], ev[:, wide(h)], v2[:, wide(h)]], axis=0
             )
-            o, lse = attend(qf[pl.ds(0, HALF), wide(h)], keys, vals, bias_f[pl.ds(0, HALF), :])
+            o, lse = attend(qf[pl.ds(0, HALF), wide(h)], keys, vals, bias_r[pl.ds(1, 1), :])
             lse_send[2, g, pl.ds(u, 1), :] = jnp.where(
                 kv | (lane >= HALF), HIDDEN, to_row(lse, eyes[0])
             )
@@ -551,7 +552,11 @@
                 lse_recv[1, step, pl.ds(u, 1), :], lse_recv[2, step, pl.ds(u, 1), :]
             )
             there = jnp.concatenate(
-                [to_column(f_lse, eye), to_column(lse_recv[0, step, pl.ds(u, 1), :], eye)], axis=0
+                [
+                    to_column(f_lse + for_me[pl.ds(0, 1), :], eye),
+                    to_column(lse_recv[0, step, pl.ds(u, 1), :] + for_me[pl.ds(1, 1), :], eye),
+                ],
+                axis=0,
             )
             here = s_loc[h]
             s = scores(q2[:, wide(h)], keys, bias_a[...]) * C2
@@ -570,6 +575,37 @@
                 sums[side, pl.ds(h, 1), :] = to_row(lse[rows], eye)
         return g
 
+    def drained():
+        id_sib.wait_send()
+        for cp in sib_sends:
+            cp.wait_send()
+
+        @pl.when(has_right)
+        def _():
+            for cp in id_right:
+                cp.wait_send()
+
+            @pl.when(core == 1)
+            def _():
+                for cp in e_copies():
+                    cp.wait_send()
+
+            def drain(h, _):
+                m_copy(h).wait_send()
+                l_copy(1, h).wait_send()
+                l_copy(0, h).wait_send()
+                return 0
+
+            lax.fori_loop(0, nh, drain, 0)
+            for i in range(3):
+                for g in range(ng):
+                    lse_copy(i, g).wait_send()
+
+        @pl.when(has_left)
+        def _():
+            for q in q_order:
+                q_copy(*q).wait_send()
+
     for g in range(no):
         lax.fori_loop(0, OG // QG, finish_heads, g)
         put(g, 0, begin)
@@ -579,39 +615,7 @@
     far_sum = remote(sums.at[other], sum_ref.at[core], sum_ss.at[1], sum_rs, sib)
     own_sum.start()
     far_sum.start()
-
-    id_sib.wait_send()
-    for cp in sib_sends:
-        cp.wait_send()
-
-    @pl.when(has_right)
-    def _():
-        for cp in id_right:
-            cp.wait_send()
-
-        e_copy(0).wait_send()
-        e_copy(1).wait_send()
-
-        def drain(h, _):
-            m_copy(h).wait_send()
-            l_copy(1, h).wait_send()
-            l_copy(0, h).wait_send()
-            return 0
-
-        lax.fori_loop(0, nh, drain, 0)
-        for i in range(3):
-            for g in range(ng):
-                lse_copy(i, g).wait_send()
-
-    @pl.when(has_left)
-    def _():
-        for cp in id_left:
-            cp.wait_send()
-        for i in range(3 * ng):
-
-            @pl.when(prompt | (i >= PUMP - TWO))
-            def _():
-                q_copy(i // ng, i % ng).wait_send()
+    drained()
 
     for g in range(no):
         put(g, 0, sent)
@@ -623,10 +627,10 @@
     arrived(sum_ref.at[other], sum_rs)
 
 
-CHUNKS = 8
-
-
-def finish(nh, out_in, sum_in, out_ref, sum_ref, sem):
+CHUNKS = 4
+
+
+def finish(nh, out_in, sum_in, out_ref, sum_ref, hold, sem):
     size = out_in.shape[0] // CHUNKS
     cps = [
         pltpu.make_async_copy(
@@ -634,10 +638,12 @@
         )
         for i in range(CHUNKS)
     ]
-    for cp in cps:
+    cps.append(pltpu.make_async_copy(hold, sum_ref, sem.at[CHUNKS]))
+    for cp in cps[:-1]:
         cp.start()
     for i in range(2):
-        sum_ref[pl.ds(i * nh, nh), :] = sum_in[i, pl.ds(0, nh), :]
+        hold[pl.ds(i * nh, nh), :] = sum_in[i, pl.ds(0, nh), :]
+    cps[-1].start()
     for cp in cps:
         cp.wait()
 
@@ -652,7 +658,7 @@
     pad = -(-nh // 8) * 8
     dma = pltpu.SemaphoreType.DMA
     scratch = [
-        pltpu.VMEM((6, 1, T), jnp.int32),
+        pltpu.VMEM((4, 1, T), jnp.int32),
         pltpu.VMEM((2 * T, w), BF16),
         pltpu.VMEM((2 * T, w), BF16),
         pltpu.VMEM((2 * T, w), BF16),
@@ -666,24 +672,24 @@
         pltpu.VMEM((2, nh, HALF, D), BF16),
         pltpu.VMEM((3, ng, 8, T), F32),
         pltpu.VMEM((3, ng, 8, T), F32),
-        pltpu.VMEM((G, 2 * T), F32),
-        pltpu.VMEM((T, 3 * T), F32),
+        pltpu.VMEM((8, 3 * T), F32),
         pltpu.VMEM((2 * T, 3 * T), F32),
         pltpu.VMEM((2 * T, HALF), F32),
+        pltpu.VMEM((8, T), F32),
         pltpu.VMEM((nh, 2 * T, D), F32),
         pltpu.VMEM((nh, 2 * T, D), F32),
         pltpu.VMEM((2, T, w), BF16),
         pltpu.VMEM((2, pad, T), F32),
         pltpu.SemaphoreType.REGULAR,
-        dma((5,)),
-        dma((6,)),
+        dma((3,)),
+        dma((4,)),
         dma((4,)),
         dma((3,)),
         dma((3,)),
+        dma((2, 2)),
         dma((2,)),
-        dma((2,)),
-        dma((3, ng)),
-        dma((3, ng)),
+        dma((3, nh)),
+        dma((3, nh)),
         dma((nh,)),
         dma((nh,)),
         dma((2, nh)),
@@ -697,6 +703,7 @@
     ]
     anywhere = pl.BlockSpec(memory_space=pl.ANY)
     vmem = pl.BlockSpec(memory_space=pltpu.VMEM)
+    operands = (queries, keys, values, segment_ids.reshape(1, T))
     out, sums = pl.pallas_call(
         functools.partial(kernel, n, ncp, nh),
         out_shape=(
@@ -707,12 +714,12 @@
         out_specs=(anywhere, anywhere),
         scratch_shapes=scratch,
         compiler_params=pltpu.CompilerParams(
-            collective_id=0, has_side_effects=True, vmem_limit_bytes=53 * 2**20
+            collective_id=0, has_side_effects=True, vmem_limit_bytes=48 * 2**20
         ),
         cost_estimate=pl.CostEstimate(
             flops=heads * T * T * D * 20, bytes_accessed=8 * T * width, transcendentals=0
         ),
-    )(queries, keys, values, segment_ids.reshape(1, T))
+    )(*[pltpu.with_memory_space_constraint(a, pltpu.HBM) for a in operands])
     return pl.pallas_call(
         functools.partial(finish, nh),
         out_shape=(
@@ -720,8 +727,8 @@
             jax.ShapeDtypeStruct((heads, T), F32),
         ),
         in_specs=[anywhere, vmem],
-        out_specs=(anywhere, vmem),
-        scratch_shapes=[dma((CHUNKS,))],
+        out_specs=(anywhere, anywhere),
+        scratch_shapes=[pltpu.VMEM((heads, T), F32), dma((CHUNKS + 1,))],
         compiler_params=pltpu.CompilerParams(vmem_limit_bytes=48 * 2**20),
     )(out, sums)
 

time: 42.9 us -> 41.4 us (0.965)
  Pallas kernels: 40.9 us -> 40.1 us
  local copies, waits for them, and re-layouts: 0.65 us -> 0 us
    unnamed x2 -> x0, local copies, waits for them, and re-layouts: 0.65 us -> none
    pallas_call x1, Pallas kernels: 1.54 us -> 0.92 us  [shards(): pl.pallas_call(functools.partial(finish, nh), out_shape=(jax.ShapeDtypeSt...]
where the time goes in v4:
time: 41.4 us; the launch traced here: 40.8 us
  Pallas kernels  40.1 us (97%)
  between operations  0.64 us (2%)
    pallas_call x1, Pallas kernels, shards(): pl.pallas_call(functools.partial(kernel, n, ncp, nh), out_shape=(jax.Shap...  39.2 us
    pallas_call x1, Pallas kernels, shards(): pl.pallas_call(functools.partial(finish, nh), out_shape=(jax.ShapeDtypeSt...  0.92 us

profile of v4, /device:TPU:6, one launch (start us, length us, event | category | flops | bytes accessed | tf_op | source)
XLA Modules:
  0.0 40.8 jit_solution(9063369104164338010)
XLA Ops:
  0.6 39.2 %shard_map.59 = (bf16[128,3072]{1,0:T(8,128)(2,1)S(1)}, f32[2,16,128]{2,1,0:T(8,128)S(1)}) custom-call(bf16[128,3072]{1,0:T(8,128)(2,1)} %q_ref.1, bf16[128,3072]{1,0:T(8,128)(2,1)} %k_ref.1, bf16[128,3072]{1,0:T(8,128)(2,1)} %v_ref.1, s32[1,128]{1,0:T(1,128)} %bitcast.1), custom_call_target="tpu_custom_call" | custom-call | flops 1006632960 | bytes 3145728 | tf_op jit(solution)/shard_map/pallas_call | solution.py:707
  39.9 0.9 %shard_map.60 = (bf16[128,3072]{1,0:T(8,128)(2,1)}, f32[24,128]{1,0:T(8,128)}) custom-call(bf16[128,3072]{1,0:T(8,128)(2,1)S(1)} %get-tuple-element.4.out_in, f32[2,16,128]{2,1,0:T(8,128)S(1)} %get-tuple-element.5.sum_in), custom_call_target="tpu_custom_call" | custom-call | tf_op jit(solution)/shard_map/pallas_call | solution.py:723

commit v5 on v4

--- a/solution.py
+++ b/solution.py
@@ -23,7 +23,7 @@
 BF16 = jnp.bfloat16
 
 QG = 2
-OG = 4
+OG = 2
 LINE = 16
 AHEAD = 6
 TWO = 2
@@ -82,6 +82,7 @@
     bias_o,
     bias_a,
     for_me,
+    l_col,
     o_loc,
     s_loc,
     stage,
@@ -451,6 +452,13 @@
 
     lax.fori_loop(0, ng, step_f1, 0)
 
+    def weights_of(g):
+        for u in range(QG):
+            upper = to_column(lse_recv[1, g, pl.ds(u, 1), :] + for_me[pl.ds(0, 1), :], eyes[1])
+            second = to_column(lse_recv[0, g, pl.ds(u, 1), :] + for_me[pl.ds(1, 1), :], eye)
+            column = jnp.concatenate([upper, second], axis=0)
+            l_col[g * QG + u] = jnp.broadcast_to(column, (T + HALF, D))
+
     def step_f0(g, _):
         @pl.when(prompt)
         def _():
@@ -462,6 +470,8 @@
 
         @pl.when(has_left)
         def _():
+            arrived(lse_recv.at[0, g], lse_rs.at[0, g])
+            arrived(lse_recv.at[1, g], lse_rs.at[1, g])
             for u in range(QG):
                 arrived(l_recv.at[1, g * QG + u], l_rs.at[1, g * QG + u])
 
@@ -491,6 +501,10 @@
         def _():
             lse_copy(2, g).start()
 
+        @pl.when(jnp.logical_not(ends))
+        def _():
+            weights_of(g)
+
         return 0
 
     lax.fori_loop(0, ng, step_f0, 0)
@@ -498,6 +512,7 @@
     @pl.when(ends)
     def _():
         def step_own(g, _):
+            weights_of(g)
             for u in range(QG):
                 own(g * QG + u, *near(g * QG + u))
             return 0
@@ -525,12 +540,6 @@
             cp.wait_send()
         else:
             cp.wait()
-
-    @pl.when(has_left)
-    def _():
-        for i in range(2):
-            for g in range(ng):
-                arrived(lse_recv.at[i, g], lse_rs.at[i, g])
 
     def finish_heads(i, g):
         step = g * (OG // QG) + i
@@ -548,16 +557,10 @@
             keys = jnp.concatenate([low[:PART], mid[:PART]], axis=0)
             vals = jnp.concatenate([low[PART:], mid[PART:]], axis=0)
             theirs = jnp.concatenate([low, mid, m_recv[h], jnp.zeros((T - G, D), BF16)], axis=0)
-            f_lse = jnp.maximum(
-                lse_recv[1, step, pl.ds(u, 1), :], lse_recv[2, step, pl.ds(u, 1), :]
+            lower = to_column(
+                lse_recv[2, step, pl.ds(u, 1), :] + for_me[pl.ds(0, 1), :], eyes[0]
             )
-            there = jnp.concatenate(
-                [
-                    to_column(f_lse + for_me[pl.ds(0, 1), :], eye),
-                    to_column(lse_recv[0, step, pl.ds(u, 1), :] + for_me[pl.ds(1, 1), :], eye),
-                ],
-                axis=0,
-            )
+            there = jnp.concatenate([jnp.broadcast_to(lower, (HALF, D)), l_col[h]], axis=0)
             here = s_loc[h]
             s = scores(q2[:, wide(h)], keys, bias_a[...]) * C2
             top = jnp.maximum(jnp.max(s, axis=1, keepdims=True), there)
@@ -676,6 +679,7 @@
         pltpu.VMEM((2 * T, 3 * T), F32),
         pltpu.VMEM((2 * T, HALF), F32),
         pltpu.VMEM((8, T), F32),
+        pltpu.VMEM((nh, T + HALF, D), F32),
         pltpu.VMEM((nh, 2 * T, D), F32),
         pltpu.VMEM((nh, 2 * T, D), F32),
         pltpu.VMEM((2, T, w), BF16),

time: 41.4 us -> 40.7 us (0.983)
  Pallas kernels: 40.1 us -> 39.5 us
    pallas_call x1, Pallas kernels: 39.2 us -> 38.6 us  [shards(): pl.pallas_call(functools.partial(kernel, n, ncp, nh), out_shape=(jax.Shap...]
where the time goes in v5:
time: 40.7 us; the launch traced here: 40.1 us
  Pallas kernels  39.5 us (97%)
  between operations  0.64 us (2%)
    pallas_call x1, Pallas kernels, shards(): pl.pallas_call(functools.partial(kernel, n, ncp, nh), out_shape=(jax.Shap...  38.6 us
    pallas_call x1, Pallas kernels, shards(): pl.pallas_call(functools.partial(finish, nh), out_shape=(jax.ShapeDtypeSt...  0.92 us

profile of v5, /device:TPU:6, one launch (start us, length us, event | category | flops | bytes accessed | tf_op | source)
XLA Modules:
  0.0 40.1 jit_solution(17348451771649142278)
XLA Ops:
  0.6 38.6 %shard_map.59 = (bf16[128,3072]{1,0:T(8,128)(2,1)S(1)}, f32[2,16,128]{2,1,0:T(8,128)S(1)}) custom-call(bf16[128,3072]{1,0:T(8,128)(2,1)} %q_ref.1, bf16[128,3072]{1,0:T(8,128)(2,1)} %k_ref.1, bf16[128,3072]{1,0:T(8,128)(2,1)} %v_ref.1, s32[1,128]{1,0:T(1,128)} %bitcast.1), custom_call_target="tpu_custom_call" | custom-call | flops 1006632960 | bytes 3145728 | tf_op jit(solution)/shard_map/pallas_call | solution.py:711
  39.2 0.9 %shard_map.60 = (bf16[128,3072]{1,0:T(8,128)(2,1)}, f32[24,128]{1,0:T(8,128)}) custom-call(bf16[128,3072]{1,0:T(8,128)(2,1)S(1)} %get-tuple-element.4.out_in, f32[2,16,128]{2,1,0:T(8,128)S(1)} %get-tuple-element.5.sum_in), custom_call_target="tpu_custom_call" | custom-call | tf_op jit(solution)/shard_map/pallas_call | solution.py:727

commit v6 on v5

--- a/solution.py
+++ b/solution.py
@@ -350,7 +350,7 @@
 
         return 0
 
-    lax.fori_loop(0, nh, step_g, 0)
+    lax.fori_loop(0, nh, step_g, 0, unroll=2)
 
     @pl.when(waits & has_left)
     def _():
@@ -507,7 +507,7 @@
 
         return 0
 
-    lax.fori_loop(0, ng, step_f0, 0)
+    lax.fori_loop(0, ng, step_f0, 0, unroll=2)
 
     @pl.when(ends)
     def _():

time: 40.7 us -> 40.7 us (level)
  no operation moved by 1% of the time
where the time goes in v6:
time: 40.7 us; the launch traced here: 40.1 us
  Pallas kernels  39.5 us (97%)
  between operations  0.64 us (2%)
    pallas_call x1, Pallas kernels, shards(): pl.pallas_call(functools.partial(kernel, n, ncp, nh), out_shape=(jax.Shap...  38.5 us
    pallas_call x1, Pallas kernels, shards(): pl.pallas_call(functools.partial(finish, nh), out_shape=(jax.ShapeDtypeSt...  0.92 us

profile of v6, /device:TPU:6, one launch (start us, length us, event | category | flops | bytes accessed | tf_op | source)
XLA Modules:
  0.0 40.1 jit_solution(12395356331183216397)
XLA Ops:
  0.6 38.5 %shard_map.59 = (bf16[128,3072]{1,0:T(8,128)(2,1)S(1)}, f32[2,16,128]{2,1,0:T(8,128)S(1)}) custom-call(bf16[128,3072]{1,0:T(8,128)(2,1)} %q_ref.1, bf16[128,3072]{1,0:T(8,128)(2,1)} %k_ref.1, bf16[128,3072]{1,0:T(8,128)(2,1)} %v_ref.1, s32[1,128]{1,0:T(1,128)} %bitcast.1), custom_call_target="tpu_custom_call" | custom-call | flops 1006632960 | bytes 3145728 | tf_op jit(solution)/shard_map/pallas_call | solution.py:711
  39.2 0.9 %shard_map.60 = (bf16[128,3072]{1,0:T(8,128)(2,1)}, f32[24,128]{1,0:T(8,128)}) custom-call(bf16[128,3072]{1,0:T(8,128)(2,1)S(1)} %get-tuple-element.4.out_in, f32[2,16,128]{2,1,0:T(8,128)S(1)} %get-tuple-element.5.sum_in), custom_call_target="tpu_custom_call" | custom-call | tf_op jit(solution)/shard_map/pallas_call | solution.py:727
